TPU v7x, 32 devices: a whole 2x2x4 slice. The times are simulated.
32 devices in a mesh: rep: 2 (over y), slab: 4 (over x, core), head: 4 (over z).
Axes of the slice: x: 2, y: 2, z: 4, core: 2. Of those that a mesh axis runs over, the one named last changes fastest.
Arguments:
- atom_feats: bfloat16 [32768, 512], P(('rep', 'slab', 'head')), parts along dimension 0, may hold values from -56 to 56
- w_qkv: bfloat16 [512, 16, 96], replicated, may hold values from -0.5 to 0.5
- w_out: bfloat16 [512, 512], replicated, may hold values from -0.25 to 0.25
- neighbours: int32 [256, 8], P(('rep', 'slab')), parts along dimension 0, may hold values from 0 to 127, as said below
- counts: int32 [256], P('rep'), parts along dimension 0, may hold values from 32 to 128, as said below
- d_out: bfloat16 [32768, 512], P(('rep', 'slab', 'head')), parts along dimension 0, may hold values from -6 to 6
Outputs:
- layer_out: bfloat16 [32768, 512], P(('rep', 'slab', 'head')), parts along dimension 0
- grad_x: bfloat16 [32768, 512], P(('rep', 'slab', 'head')), parts along dimension 0
- grad_wo: float32 [1024, 512], P(('rep', 'head'), 'slab'), parts along dimension 0
There are 2 independent parts, one for each index of `rep`. A program takes and returns all parts, laid end to end along the dimension named above; an argument that names none is the same for every part. Nothing has to cross between parts.
Inputs may be any that keep to these rules, and one draw needn't show every extreme that they name: `neighbours`: row b lists 8 different blocks, b itself first; every other listed block lies at most 16 positions from b in the cyclic order of the 128 blocks, and the last entry lies exactly 16 positions away. `counts`: in every aligned group of four blocks one block holds 128 atoms and another 128 // 4.
All inputs are finite; a program needn't handle non-finite values.
Results may differ from a plain program's by a relative error of at most 0.014.
The roundings to bfloat16 on the way count: a program that leaves them out, or rounds other values in their place, can miss the bound.
Values may be sent and summed in bfloat16 or wider, within the bound.
A program may use at most 128 MiB of HBM per device.

v0:
```python
import math

import jax
import jax.numpy as jnp
from jax import lax
from jax.sharding import PartitionSpec as P

BLOCK = 128
NEIGH = 8
REACH = 16


def padded(shard, sides, width):
    for axis, dim in sides:
        count, length = (lax.axis_size(axis), shard.shape[dim])
        up = [(i, (i + 1) % count) for i in range(count)]
        down = [(j, i) for i, j in up]
        last = lax.slice_in_dim(shard, length - width, length, axis=dim)
        leading = lax.slice_in_dim(shard, 0, width, axis=dim)
        before = lax.ppermute(last, axis, up)
        after = lax.ppermute(leading, axis, down)
        shard = jnp.concatenate([before, shard, after], axis=dim)
    return shard


def from_behind(shard, axis, by):
    count = lax.axis_size(axis)
    return lax.ppermute(shard, axis, [(i, (i + by) % count) for i in range(count)])


def lookup_counts(block_ids, counts):
    table_ids = jnp.arange(counts.shape[0], dtype=jnp.int32)
    hits = block_ids[..., None] == table_ids
    return jnp.sum(jnp.where(hits, counts, 0), axis=-1)


def on_device(atom_feats, w_qkv, w_out, neighbours, counts, d_out):
    row_count, model_width = atom_feats.shape
    n_head = lax.axis_size("head")
    n_slab = lax.axis_size("slab")
    heads_all = w_qkv.shape[1]
    head_dim = w_qkv.shape[2] // 3
    own_heads = heads_all // n_head
    slab_blocks = neighbours.shape[0]
    slab_rows = row_count * n_head
    total_blocks = slab_blocks * n_slab
    total_atoms = slab_rows * n_slab
    head_index = lax.axis_index("head")
    slab_index = lax.axis_index("slab")
    scale = 1.0 / math.sqrt(head_dim)
    w_own = lax.dynamic_slice_in_dim(w_qkv, head_index * own_heads, own_heads, 1).reshape(
        model_width, own_heads * 3 * head_dim
    )
    qkv_heads = jnp.dot(
        lax.all_gather(atom_feats, "head", axis=0, tiled=True),
        w_own,
        preferred_element_type=jnp.float32,
    ).astype(jnp.bfloat16)
    qkv_heads = qkv_heads.reshape(slab_blocks, BLOCK, own_heads, 3 * head_dim)
    qkv_slots = jnp.transpose(qkv_heads, (0, 2, 3, 1))
    queries = qkv_slots[:, :, :head_dim, :]
    keyvals = qkv_slots[:, :, head_dim:, :]
    kv_ext = padded(keyvals, (("slab", 0),), REACH)
    slot_pos = jnp.arange(BLOCK, dtype=jnp.int32)
    local_lists = (neighbours - slab_index * slab_blocks + REACH) % total_blocks
    list_counts = lookup_counts(neighbours, counts)
    key_valid = (slot_pos[None, None, :] < list_counts[..., None]).reshape(
        slab_blocks, NEIGH * BLOCK
    )
    group = min(slab_blocks, max(1, 512 // BLOCK))
    n_groups = slab_blocks // group
    query_groups = queries.reshape(n_groups, group, own_heads, head_dim, BLOCK)
    list_groups = local_lists.reshape(n_groups, group, NEIGH)
    valid_groups = key_valid.reshape(n_groups, group, NEIGH * BLOCK)

    def gather_keys(lists):
        picked = kv_ext[lists]
        return (picked[:, :, :, :head_dim, :], picked[:, :, :, head_dim:, :])

    def raw_scores(query_block, key_block, valid):
        scores = (
            jnp.einsum(
                "ghdq,gnhdk->ghqnk", query_block, key_block, preferred_element_type=jnp.float32
            )
            * scale
        )
        scores = scores.reshape(group, own_heads, BLOCK, NEIGH * BLOCK)
        return jnp.where(valid[:, None, None, :], scores, -jnp.inf)

    def forward_group(inputs):
        query_block, lists, valid = inputs
        key_block, value_block = gather_keys(lists)
        scores = raw_scores(query_block, key_block, valid)
        top = jnp.max(scores, axis=-1, keepdims=True)
        log_total = top + jnp.log(jnp.sum(jnp.exp(scores - top), axis=-1, keepdims=True))
        probs = jnp.exp(scores - log_total).astype(jnp.bfloat16)
        probs = probs.reshape(group, own_heads, BLOCK, NEIGH, BLOCK)
        attended = jnp.einsum(
            "ghqnk,gnhdk->gqhd", probs, value_block, preferred_element_type=jnp.float32
        )
        return (attended.astype(jnp.bfloat16), log_total)

    attended, log_totals = lax.map(forward_group, (query_groups, list_groups, valid_groups))
    attn_rows = lax.all_to_all(
        attended.reshape(slab_rows, own_heads, head_dim),
        "head",
        split_axis=0,
        concat_axis=1,
        tiled=True,
    )
    attn_rows = attn_rows.reshape(row_count, model_width)
    row_global = (slab_index * n_head + head_index) * row_count + jnp.arange(
        row_count, dtype=jnp.int32
    )
    row_counts = lookup_counts(row_global // BLOCK, counts)
    row_valid = (row_global % BLOCK < row_counts)[:, None]
    projected = jnp.dot(attn_rows, w_out, preferred_element_type=jnp.float32)
    layer_out = jnp.where(row_valid, projected, jnp.zeros_like(projected)).astype(jnp.bfloat16)
    masked_grad = jnp.where(row_valid, d_out, jnp.zeros_like(d_out))
    root_atoms = math.sqrt(total_atoms)
    term = lax.dot_general(
        attn_rows, masked_grad, (((0,), (0,)), ((), ())), preferred_element_type=jnp.float32
    )
    wo_term = lax.psum_scatter(
        (term / root_atoms).astype(jnp.bfloat16), "head", scatter_dimension=0, tiled=True
    )
    d_attn = lax.dot_general(
        masked_grad, w_out, (((1,), (1,)), ((), ())), preferred_element_type=jnp.float32
    ).astype(jnp.bfloat16)
    d_heads = lax.all_to_all(
        d_attn.reshape(row_count, heads_all, head_dim),
        "head",
        split_axis=1,
        concat_axis=0,
        tiled=True,
    )
    grad_wo = lax.psum_scatter(wo_term, "slab", scatter_dimension=1, tiled=True).astype(jnp.float32)
    d_groups = d_heads.reshape(n_groups, group, BLOCK, own_heads, head_dim)

    def backward_group(carry, inputs):
        query_block, lists, valid, log_total, attended_block, grad_block = inputs
        key_block, value_block = gather_keys(lists)
        scores = raw_scores(query_block, key_block, valid)
        weights = jnp.exp(scores - log_total)
        probs = weights.astype(jnp.bfloat16).reshape(group, own_heads, BLOCK, NEIGH, BLOCK)
        delta = jnp.sum(
            grad_block.astype(jnp.float32) * attended_block.astype(jnp.float32), axis=-1
        )
        delta = jnp.transpose(delta, (0, 2, 1))[..., None]
        grad_values = jnp.einsum(
            "ghqnk,gqhd->gnhdk", probs, grad_block, preferred_element_type=jnp.float32
        )
        grad_probs = jnp.einsum(
            "gqhd,gnhdk->ghqnk", grad_block, value_block, preferred_element_type=jnp.float32
        )
        grad_probs = grad_probs.reshape(group, own_heads, BLOCK, NEIGH * BLOCK)
        grad_scores = (weights * (grad_probs - delta)).astype(jnp.bfloat16)
        grad_scores = grad_scores.reshape(group, own_heads, BLOCK, NEIGH, BLOCK)
        grad_queries = (
            jnp.einsum(
                "ghqnk,gnhdk->gqhd", grad_scores, key_block, preferred_element_type=jnp.float32
            )
            * scale
        )
        grad_keys = (
            jnp.einsum(
                "ghqnk,ghdq->gnhdk", grad_scores, query_block, preferred_element_type=jnp.float32
            )
            * scale
        )
        both = jnp.concatenate([grad_keys, grad_values], axis=3).reshape(
            group * NEIGH, own_heads, 2 * head_dim, BLOCK
        )
        carry = carry.at[lists.reshape(-1)].add(both)
        return (carry, grad_queries.astype(jnp.bfloat16))

    start_kv = jnp.zeros((slab_blocks + 2 * REACH, own_heads, 2 * head_dim, BLOCK), jnp.float32)
    grad_ext, grad_q = lax.scan(
        backward_group,
        start_kv,
        (query_groups, list_groups, valid_groups, log_totals, attended, d_groups),
    )
    lower_rim = grad_ext[:REACH]
    upper_rim = grad_ext[REACH + slab_blocks :]
    own_grad = grad_ext[REACH : REACH + slab_blocks]
    from_next = from_behind(lower_rim.astype(jnp.bfloat16), "slab", -1).astype(lower_rim.dtype)
    from_prev = from_behind(upper_rim.astype(jnp.bfloat16), "slab", 1).astype(upper_rim.dtype)
    own_grad = own_grad.at[slab_blocks - REACH :].add(from_next)
    own_grad = own_grad.at[:REACH].add(from_prev)
    own_grad = jnp.transpose(own_grad.astype(jnp.bfloat16), (0, 3, 1, 2))
    grad_qkv = jnp.concatenate(
        [grad_q.reshape(slab_blocks, BLOCK, own_heads, head_dim), own_grad], axis=-1
    )
    grad_rows = lax.all_to_all(
        grad_qkv.reshape(slab_rows, own_heads, 3 * head_dim),
        "head",
        split_axis=0,
        concat_axis=1,
        tiled=True,
    )
    grad_rows = grad_rows.reshape(row_count, heads_all * 3 * head_dim)
    flat_w = w_qkv.reshape(model_width, heads_all * 3 * head_dim)
    grad_x = lax.dot_general(
        grad_rows, flat_w, (((1,), (1,)), ((), ())), preferred_element_type=jnp.float32
    ).astype(jnp.bfloat16)
    return (layer_out, grad_x, grad_wo)


def solution(mesh):
    placed = (
        P(("rep", "slab", "head"), None),
        P(),
        P(),
        P(("rep", "slab"), None),
        P("rep"),
        P(("rep", "slab", "head"), None),
    )
    return jax.shard_map(
        on_device,
        mesh=mesh,
        in_specs=placed,
        out_specs=(
            P(("rep", "slab", "head"), None),
            P(("rep", "slab", "head"), None),
            P(("rep", "head"), "slab"),
        ),
        check_vma=False,
    )
```

profile of v0, /device:TPU:0, one launch (start us, length us, event | category | flops | bytes accessed | tf_op | source)
XLA Modules:
  0.0 743.3 jit_solution(745383937876917702)
XLA Ops:
  12.7 6.3 all-to-all-start.1
  19.1 93.8 %all-gather.2.cloned.1.call-done = bf16[4096,512]{1,0:T(8,128)(2,1)} async-done(((bf16[1024,512]{1,0:T(8,128)(2,1)}), bf16[4096,512]{1,0:T(8,128)(2,1)}) %all-gather.2.cloned.1.call-update) | async-done | bytes 4194320 | tf_op jit(solution)/shard_map/all_gather | solution.py:55
  112.8 4.0 fusion.44
  133.3 12.8 %collective-permute-done = bf16[16,4,64,128]{3,2,1,0:T(8,128)(2,1)} collective-permute-done((bf16[16,4,64,128]{3,2,1,0:T(8,128)(2,1)}, bf16[16,4,64,128]{3,2,1,0:T(8,128)(2,1)}, u32[]{:S(2)}, u32[]{:S(2)}) %collective-permute-start) | collective-permute-done | bytes 1048608 | tf_op jit(solution)/shard_map/ppermute | solution.py:20
  147.0 3.5 pad_maximum_fusion.1
  150.5 124.0 %while.26 = (s32[]{:T(128)}, bf16[8,4,128,4,32]{2,4,3,1,0:T(8,128)(2,1)}, f32[8,4,4,128,1]{3,2,1,4,0:T(4,128)S(1)}, s32[8,4,8]{2,1,0:T(4,128)S(1)}, bf16[64,4,64...) while((s32[]{:T(128)}, ...), condition=%wide.region_5.6_spmd, body=%wide.region_2.5_spmd.sunk | while | flops 291568736 | bytes 36013920 | solution.py:103
  150.6 4.3 gather_fusion
  156.9 3.6 fusion.91
  162.5 3.4 fusion.92
  166.1 4.3 gather_fusion
  172.4 3.6 fusion.91
  181.6 4.3 gather_fusion
  187.9 3.6 fusion.91
  197.1 4.3 gather_fusion
  203.4 3.6 fusion.91
  212.6 4.3 gather_fusion
  218.9 3.6 fusion.91
  228.1 4.3 gather_fusion
  234.4 3.6 fusion.91
  243.6 4.3 gather_fusion
  249.9 3.6 fusion.91
  259.1 4.3 gather_fusion
  265.4 3.6 fusion.91
  274.5 4.3 broadcast_in_dim.97
  278.8 279.6 %while.27 = (s32[]{:T(128)}, f32[64,4,64,128]{3,2,1,0:T(8,128)}, bf16[8,4,128,4,32]{2,1,0,4,3:T(4,128)(2,1)}, s32[8,4,8]{2,1,0:T(4,128)S(1)}, bf16[8,4,4,32,128]...) while((s32[]{:T(128)}, f32[64,4,64,128]{3,2,1,0:T(8,128)}, ...), condition=%wide.region_9.10_spmd, body=%wide.region_6.9_spmd.sunk | while | flops 695073984 | bytes 101137560 | solution.py:178
  278.9 4.3 gather_fusion.1
  299.2 10.0 %scatter_fusion = f32[64,4,64,128]{3,2,1,0:T(8,128)} fusion(f32[64,4,64,128]{3,2,1,0:T(8,128)} %get-tuple-element.380, s32[32]{0:T(128)S(1)} %fusion.103, f32[32,4,64,128]{3,2,1,0:T(8,128)} %bitcast.200), kind=kCustom, calls=%fused_computation.2.clone.1 | custom fusion | flops 1048576 | bytes 12583040 | tf_op jit(solution)/shard_map/while/body/eval_jaxpr/scatter-add | solution.py:174
  309.2 3.6 fusion.108
  313.7 4.3 gather_fusion.1
  334.1 10.2 %scatter_fusion = f32[64,4,64,128]{3,2,1,0:T(8,128)} fusion(f32[64,4,64,128]{3,2,1,0:T(8,128)} %get-tuple-element.380, s32[32]{0:T(128)S(1)} %fusion.103, f32[32,4,64,128]{3,2,1,0:T(8,128)} %bitcast.200), kind=kCustom, calls=%fused_computation.2.clone.1 | custom fusion | flops 1048576 | bytes 12583040 | tf_op jit(solution)/shard_map/while/body/eval_jaxpr/scatter-add | solution.py:174
  344.2 3.6 fusion.108
  348.8 4.3 gather_fusion.1
  369.1 10.1 %scatter_fusion = f32[64,4,64,128]{3,2,1,0:T(8,128)} fusion(f32[64,4,64,128]{3,2,1,0:T(8,128)} %get-tuple-element.380, s32[32]{0:T(128)S(1)} %fusion.103, f32[32,4,64,128]{3,2,1,0:T(8,128)} %bitcast.200), kind=kCustom, calls=%fused_computation.2.clone.1 | custom fusion | flops 1048576 | bytes 12583040 | tf_op jit(solution)/shard_map/while/body/eval_jaxpr/scatter-add | solution.py:174
  379.2 3.6 fusion.108
  383.8 4.3 gather_fusion.1
  404.1 10.1 %scatter_fusion = f32[64,4,64,128]{3,2,1,0:T(8,128)} fusion(f32[64,4,64,128]{3,2,1,0:T(8,128)} %get-tuple-element.380, s32[32]{0:T(128)S(1)} %fusion.103, f32[32,4,64,128]{3,2,1,0:T(8,128)} %bitcast.200), kind=kCustom, calls=%fused_computation.2.clone.1 | custom fusion | flops 1048576 | bytes 12583040 | tf_op jit(solution)/shard_map/while/body/eval_jaxpr/scatter-add | solution.py:174
  414.2 3.6 fusion.108
  418.7 4.3 gather_fusion.1
  439.1 10.1 %scatter_fusion = f32[64,4,64,128]{3,2,1,0:T(8,128)} fusion(f32[64,4,64,128]{3,2,1,0:T(8,128)} %get-tuple-element.380, s32[32]{0:T(128)S(1)} %fusion.103, f32[32,4,64,128]{3,2,1,0:T(8,128)} %bitcast.200), kind=kCustom, calls=%fused_computation.2.clone.1 | custom fusion | flops 1048576 | bytes 12583040 | tf_op jit(solution)/shard_map/while/body/eval_jaxpr/scatter-add | solution.py:174
  449.2 3.6 fusion.108
  453.7 4.3 gather_fusion.1
  474.1 10.0 %scatter_fusion = f32[64,4,64,128]{3,2,1,0:T(8,128)} fusion(f32[64,4,64,128]{3,2,1,0:T(8,128)} %get-tuple-element.380, s32[32]{0:T(128)S(1)} %fusion.103, f32[32,4,64,128]{3,2,1,0:T(8,128)} %bitcast.200), kind=kCustom, calls=%fused_computation.2.clone.1 | custom fusion | flops 1048576 | bytes 12583040 | tf_op jit(solution)/shard_map/while/body/eval_jaxpr/scatter-add | solution.py:174
  484.0 3.6 fusion.108
  488.6 4.3 gather_fusion.1
  508.9 10.1 %scatter_fusion = f32[64,4,64,128]{3,2,1,0:T(8,128)} fusion(f32[64,4,64,128]{3,2,1,0:T(8,128)} %get-tuple-element.380, s32[32]{0:T(128)S(1)} %fusion.103, f32[32,4,64,128]{3,2,1,0:T(8,128)} %bitcast.200), kind=kCustom, calls=%fused_computation.2.clone.1 | custom fusion | flops 1048576 | bytes 12583040 | tf_op jit(solution)/shard_map/while/body/eval_jaxpr/scatter-add | solution.py:174
  519.0 3.6 fusion.108
  523.5 4.3 gather_fusion.1
  543.9 10.0 %scatter_fusion = f32[64,4,64,128]{3,2,1,0:T(8,128)} fusion(f32[64,4,64,128]{3,2,1,0:T(8,128)} %get-tuple-element.380, s32[32]{0:T(128)S(1)} %fusion.103, f32[32,4,64,128]{3,2,1,0:T(8,128)} %bitcast.200), kind=kCustom, calls=%fused_computation.2.clone.1 | custom fusion | flops 1048576 | bytes 12583040 | tf_op jit(solution)/shard_map/while/body/eval_jaxpr/scatter-add | solution.py:174
  553.9 3.6 fusion.108
  558.4 4.7 convert.5
  568.9 6.7 copy.106
  578.2 6.4 reshape.337
  584.6 3.5 all-to-all-start
  590.1 3.7 add_dynamic-update-slice_fusion
  593.8 3.7 fusion.43
  602.1 7.2 copy.97
  609.3 5.3 all-to-all-done
  614.6 4.9 all-to-all-start.2
  619.5 3.6 reshape.338
  623.1 5.6 copy.92
  631.6 30.0 %reduce-scatter.5.cloned.1.call-done = bf16[128,512]{1,0:T(8,128)(2,1)} async-done(((bf16[512,512]{1,0:T(8,128)(2,1)}), bf16[128,512]{1,0:T(8,128)(2,1)}) %reduce-scatter.5.cloned.1.call-update) | async-done | bytes 131088 | tf_op jit(solution)/shard_map/reduce_scatter | solution.py:124
  665.0 58.3 %reduce-scatter.7.cloned.1.call-done = bf16[128,128]{1,0:T(8,128)(2,1)} async-done(((bf16[512,128]{1,0:T(8,128)(2,1)}), bf16[128,128]{1,0:T(8,128)(2,1)}) %reduce-scatter.7.cloned.1.call-update) | async-done | bytes 32784
  724.9 7.2 copy.99
  732.1 4.7 convolution_convert_fusion.1
  (297 shorter events, 236.7 us)
Async XLA Ops:
  7.2 11.9 %copy-start = (bf16[512,16,96]{0,2,1:T(8,128)(2,1)S(1)}, bf16[512,16,96]{0,2,1:T(8,128)(2,1)}, u32[]{:S(2)}) copy-start(bf16[512,16,96]{0,2,1:T(8,128)(2,1)} %param.15) | copy-start | bytes 4718596
  7.2 105.7 %all-gather.2.cloned.1.call-start = ((), (), s32[]{:S(2)}) async-start(), calls=%async_computation.5 | async-start | bytes 5242880 | tf_op jit(solution)/shard_map/all_gather | solution.py:55
  9.0 0.6 copy-start.7
  12.7 112.3 %all-to-all-start.1 = ((bf16[1024,16,32]{0,2,1:T(8,128)(2,1)}), bf16[1024,16,32]{0,2,1:T(8,128)(2,1)S(1)}, u32[]{:S(2)}, u32[]{:S(2)}) async-start(bf16[1024,16,32]{0,2,1:T(8,128)(2,1)} %bitcast.216), calls=%async_computation.1 | async-start | bytes 2097152 | tf_op jit(solution)/shard_map/all_to_all | solution.py:130
  117.7 6.3 copy-start.5
  117.7 6.4 copy-start.6
  118.9 1.6 copy-start.3
  122.2 23.9 %collective-permute-start = (bf16[16,4,64,128]{3,2,1,0:T(8,128)(2,1)}, bf16[16,4,64,128]{3,2,1,0:T(8,128)(2,1)}, u32[]{:S(2)}, u32[]{:S(2)}) collective-permute-start(bf16[16,4,64,128]{3,2,1,0:T(8,128)(2,1)} %get-tuple-element.218), channel_id=1, source_target_pairs={{0,4},{4,8},{8,12},{12,0},{1,5},{5,9},{9,13},{13,1},{2,6},{6,10},{... | collective-permute-start | bytes 3145736 | tf_op jit(solution)/shard_map/ppermute | solution.py:20
  122.2 24.8 %collective-permute-start.1 = (bf16[16,4,64,128]{3,2,1,0:T(8,128)(2,1)}, bf16[16,4,64,128]{3,2,1,0:T(8,128)(2,1)}, u32[]{:S(2)}, u32[]{:S(2)}) collective-permute-start(bf16[16,4,64,128]{3,2,1,0:T(8,128)(2,1)} %get-tuple-element.219), channel_id=1, source_target_pairs={{4,0},{8,4},{12,8},{0,12},{5,1},{9,5},{13,9},{1,13},{6,2},{10,6},{... | collective-permute-start | bytes 3145736 | tf_op jit(solution)/shard_map/ppermute | solution.py:21
  292.5 3.8 copy-start.1
  327.3 3.8 copy-start.1
  362.4 3.8 copy-start.1
  397.4 3.8 copy-start.1
  432.4 3.8 copy-start.1
  467.3 3.8 copy-start.1
  502.2 3.8 copy-start.1
  537.2 3.8 copy-start.1
  558.4 8.3 %copy-start.2 = (f32[64,4,64,128]{3,2,1,0:T(8,128)S(1)}, f32[64,4,64,128]{3,2,1,0:T(8,128)}, u32[]{:S(2)}) copy-start(f32[64,4,64,128]{3,2,1,0:T(8,128)} %get-tuple-element.121) | copy-start | bytes 25165828
  564.6 25.5 %collective-permute-start.2 = (bf16[16,4,64,128]{3,2,1,0:T(8,128)(2,1)}, bf16[16,4,64,128]{3,2,1,0:T(8,128)(2,1)}, u32[]{:S(2)}, u32[]{:S(2)}) collective-permute-start(bf16[16,4,64,128]{3,2,1,0:T(8,128)(2,1)} %get-tuple-element.217), channel_id=1, source_target_pairs={{0,12},{4,0},{8,4},{12,8},{1,13},{5,1},{9,5},{13,9},{2,14},{6,2},{... | collective-permute-start | bytes 3145736 | tf_op jit(solution)/shard_map/ppermute | solution.py:28
  566.6 27.2 %collective-permute-start.3 = (bf16[16,4,64,128]{3,2,1,0:T(8,128)(2,1)}, bf16[16,4,64,128]{3,2,1,0:T(8,128)(2,1)}, u32[]{:S(2)}, u32[]{:S(2)}) collective-permute-start(bf16[16,4,64,128]{3,2,1,0:T(8,128)(2,1)} %get-tuple-element.216), channel_id=1, source_target_pairs={{0,4},{4,8},{8,12},{12,0},{1,5},{5,9},{9,13},{13,1},{2,6},{6,10},{... | collective-permute-start | bytes 3145736 | tf_op jit(solution)/shard_map/ppermute | solution.py:28
  584.6 30.0 %all-to-all-start = ((bf16[4,2,65536]{2,1,0:T(2,128)(2,1)}), bf16[4,2,65536]{2,1,0:T(2,128)(2,1)S(1)}, u32[]{:S(2)}, u32[]{:S(2)}) async-start(bf16[4,2,65536]{2,1,0:T(2,128)(2,1)} %reshape.337), calls=%async_computation | async-start | bytes 2097152 | tf_op jit(solution)/shard_map/all_to_all | solution.py:104
  597.5 2.6 copy-start.4
  614.6 110.3 %all-to-all-start.2 = ((bf16[4096,4,96]{2,1,0:T(4,128)(2,1)}), bf16[4096,4,96]{2,1,0:T(4,128)(2,1)}, u32[]{:S(2)}, u32[]{:S(2)}) async-start(bf16[4096,4,96]{2,1,0:T(4,128)(2,1)} %copy.97), calls=%async_computation.2 | async-start | bytes 8388608 | tf_op jit(solution)/shard_map/all_to_all | solution.py:194
  619.4 9.2 %copy-start.8 = (pred[1024]{0:T(1024)(128)(4,1)S(1)}, pred[1024]{0:T(1024)(128)(4,1)}, u32[]{:S(2)}) copy-start(pred[1024]{0:T(1024)(128)(4,1)} %copy-done.7) | copy-start | bytes 3076
  619.5 42.2 %reduce-scatter.5.cloned.1.call-start = ((), (), s32[]{:S(2)}) async-start(), calls=%async_computation.6 | async-start | bytes 655360 | tf_op jit(solution)/shard_map/reduce_scatter | solution.py:124
  623.1 40.2 %copy-start.9 = (bf16[512,512]{1,0:T(8,128)(2,1)S(1)}, bf16[512,512]{1,0:T(8,128)(2,1)}, u32[]{:S(2)}) copy-start(bf16[512,512]{1,0:T(8,128)(2,1)} %param.16) | copy-start | bytes 1572868
  631.5 91.8 %reduce-scatter.7.cloned.1.call-start = ((), (), s32[]{:S(2)}) async-start(), calls=%async_computation.7 | async-start | bytes 163840
Sparse Core Ops, SparseCore 0:
  9.6 103.2 all-gather.1
  631.6 29.9 reduce-scatter.4
  664.6 58.6 reduce-scatter.6
where the time goes:
time: 749 us; the launch traced here: 743 us
  waiting for transfers between devices  204 us (27%)
  local copies, waits for them, and re-layouts  201 us (27%)
  matrix products  175 us (23%)
  other arithmetic  130 us (17%)
  starting transfers between devices  18.6 us (2%)
  between operations  14 us (2%)
    all_gather x1, waiting for transfers between devices, on_device(): lax.all_gather(atom_feats, 'head', axis=0, tiled=True)  93.8 us
    scatter-add x8, other arithmetic, backward_group(): carry = carry.at[lists.reshape(-1)].add(both)  80.5 us
    gather x16, local copies, waits for them, and re-layouts, gather_keys(): picked = kv_ext[lists]  69.3 us
    unnamed x4, waiting for transfers between devices  59 us
    dot_general x16, matrix products, raw_scores(): jnp.einsum('ghdq,gnhdk->ghqnk', query_block, key_block, preferred_element...  46.6 us
    slice x16, local copies, waits for them, and re-layouts, gather_keys(): return (picked[:, :, :, :head_dim, :], picked[:, :, :, head_dim:, :])  31 us
    reduce_scatter x1, waiting for transfers between devices, on_device(): lax.psum_scatter((term / root_atoms).astype(jnp.bfloat16), 'head', scatte...  30 us
    dot_general x8, matrix products, backward_group(): jnp.einsum('ghqnk,gnhdk->gqhd', grad_scores, key_block, preferred_element...  29.1 us
  transfers between devices with their start and end apart: 10, of which 7 were waited for; matrix products, arithmetic and copies ran while one was open for 10% of the time, Pallas kernels for 0%

commit v1 on v0

v1 whole, which is shorter than its diff:
```python
import functools
import math

import jax
import jax.numpy as jnp
from jax import lax
from jax.experimental import pallas as pl
from jax.experimental.pallas import tpu as pltpu
from jax.sharding import PartitionSpec as P

BLOCK = 128
NEIGH = 8
REACH = 16
VMEM_BYTES = 48 * 1024 * 1024


def from_behind(shard, axis, by):
    count = lax.axis_size(axis)
    return lax.ppermute(shard, axis, [(i, (i + by) % count) for i in range(count)])


def lookup_counts(block_ids, counts):
    table_ids = jnp.arange(counts.shape[0], dtype=jnp.int32)
    hits = block_ids[..., None] == table_ids
    return jnp.sum(jnp.where(hits, counts, 0), axis=-1)


def dot(a, b, dims):
    return lax.dot_general(a, b, (dims, ((), ())), preferred_element_type=jnp.float32)


def project_kernel(x_ref, g_ref, w_ref, wo_ref, out_ref):
    width = wo_ref.shape[0]
    qkv = dot(x_ref[...], w_ref[0], ((1,), (0,)))
    out_ref[0, :, : 3 * width] = qkv.astype(jnp.bfloat16)
    d_attn = dot(g_ref[...], wo_ref[...], ((1,), (1,)))
    out_ref[0, :, 3 * width :] = d_attn.astype(jnp.bfloat16)


def attention_kernel(
    heads, lists, list_counts, own_ref, kv_ref, att_ref, dq_ref, dkv_ref, s_ref, p_ref, g_ref
):
    step = pl.program_id(0)
    width = att_ref.shape[2]
    head_dim = width // heads
    lanes = heads * BLOCK
    scale = 1.0 / math.sqrt(head_dim)
    exp_scale = scale * math.log2(math.e)

    @pl.when(step == 0)
    def _():
        dkv_ref[...] = jnp.zeros_like(dkv_ref)

    row_head = lax.broadcasted_iota(jnp.int32, (width, lanes), 0) // head_dim
    lane_head = lax.broadcasted_iota(jnp.int32, (width, lanes), 1) // BLOCK
    diagonal = row_head == lane_head

    def spread(rows):
        turned = rows.astype(jnp.float32).T
        return jnp.where(diagonal, jnp.concatenate([turned] * heads, axis=1), 0.0)

    def gather_diagonal(full):
        parts = [
            full[h * head_dim : (h + 1) * head_dim, h * BLOCK : (h + 1) * BLOCK]
            for h in range(heads)
        ]
        return jnp.concatenate(parts, axis=0).T

    own = own_ref[0]
    q_bd = spread(own[:, :width]).astype(jnp.bfloat16)
    grad_bd = spread(own[:, 3 * width :])
    slots = lax.broadcasted_iota(jnp.int32, (BLOCK, 1), 0)
    ids = [lists[step * NEIGH + n] for n in range(NEIGH)]

    top = jnp.full((8, lanes), -jnp.inf, jnp.float32)
    for n in range(NEIGH):
        scores = dot(kv_ref[ids[n], :, :width], q_bd, ((1,), (0,)))
        scores = jnp.where(slots < list_counts[step * NEIGH + n], scores, -jnp.inf)
        s_ref[n] = scores
        top = jnp.maximum(top, jnp.max(scores.reshape(BLOCK // 8, 8, lanes), axis=0))
    top = jnp.max(top, axis=0, keepdims=True) * exp_scale

    total = jnp.zeros((8, lanes), jnp.float32)
    for n in range(NEIGH):
        p = jnp.exp2(s_ref[n] * exp_scale - top)
        total += jnp.sum(p.reshape(BLOCK // 8, 8, lanes), axis=0)
        p_ref[n * BLOCK : (n + 1) * BLOCK] = p.astype(jnp.bfloat16)
    inverse = 1.0 / jnp.sum(total, axis=0, keepdims=True)

    values = jnp.concatenate([kv_ref[ids[n], :, width:] for n in range(NEIGH)], axis=0)
    att_full = dot(values, p_ref[...], ((0,), (0,))) * inverse
    att_round = att_full.astype(jnp.bfloat16)
    att_ref[0] = gather_diagonal(att_full).astype(jnp.bfloat16)

    grad_bd = (grad_bd * inverse).astype(jnp.bfloat16)
    delta = jnp.sum(
        grad_bd.astype(jnp.float32) * att_round.astype(jnp.float32), axis=0, keepdims=True
    )
    for n in range(NEIGH):
        at = slice(n * BLOCK, (n + 1) * BLOCK)
        grad_probs = dot(kv_ref[ids[n], :, width:], grad_bd, ((1,), (0,)))
        p = p_ref[at]
        grad_scores = (p.astype(jnp.float32) * (grad_probs - delta)).astype(jnp.bfloat16)
        g_ref[at] = grad_scores
        dkv_ref[ids[n], :, :width] += dot(grad_scores, q_bd, ((1,), (1,))) * scale
        dkv_ref[ids[n], :, width:] += dot(p, grad_bd, ((1,), (1,)))

    keys = jnp.concatenate([kv_ref[ids[n], :, :width] for n in range(NEIGH)], axis=0)
    dq_full = dot(keys, g_ref[...], ((0,), (0,))) * scale
    dq_ref[0] = gather_diagonal(dq_full).astype(jnp.bfloat16)


def on_device(atom_feats, w_qkv, w_out, neighbours, counts, d_out):
    row_count, model_width = atom_feats.shape
    n_head = lax.axis_size("head")
    n_slab = lax.axis_size("slab")
    heads_all = w_qkv.shape[1]
    head_dim = w_qkv.shape[2] // 3
    own_heads = heads_all // n_head
    width = own_heads * head_dim
    slab_blocks = neighbours.shape[0]
    slab_rows = row_count * n_head
    total_blocks = slab_blocks * n_slab
    total_atoms = slab_rows * n_slab
    ext_blocks = slab_blocks + 2 * REACH
    head_index = lax.axis_index("head")
    slab_index = lax.axis_index("slab")
    bf16 = jnp.bfloat16

    row_global = (slab_index * n_head + head_index) * row_count + jnp.arange(
        row_count, dtype=jnp.int32
    )
    row_counts = lookup_counts(row_global // BLOCK, counts)
    row_valid = (row_global % BLOCK < row_counts)[:, None]
    masked_grad = jnp.where(row_valid, d_out, jnp.zeros_like(d_out))
    w_groups = jnp.transpose(
        w_qkv.reshape(model_width, n_head, own_heads, 3, head_dim), (1, 0, 3, 2, 4)
    ).reshape(n_head, model_width, 3 * width)

    projected = pl.pallas_call(
        project_kernel,
        grid=(n_head,),
        in_specs=[
            pl.BlockSpec((row_count, model_width), lambda g: (0, 0)),
            pl.BlockSpec((row_count, model_width), lambda g: (0, 0)),
            pl.BlockSpec((1, model_width, 3 * width), lambda g: (g, 0, 0)),
            pl.BlockSpec((width, model_width), lambda g: (g, 0)),
        ],
        out_specs=pl.BlockSpec((1, row_count, 4 * width), lambda g: (g, 0, 0)),
        out_shape=jax.ShapeDtypeStruct((n_head, row_count, 4 * width), bf16),
        compiler_params=pltpu.CompilerParams(vmem_limit_bytes=VMEM_BYTES),
    )(atom_feats, masked_grad, w_groups, w_out)
    own = lax.all_to_all(projected, "head", split_axis=0, concat_axis=0, tiled=True)
    own = own.reshape(slab_blocks, BLOCK, 4 * width)

    keyvals = own[:, :, width : 3 * width]
    before = from_behind(keyvals[slab_blocks - REACH :], "slab", 1)
    after = from_behind(keyvals[:REACH], "slab", -1)
    kv_ext = jnp.concatenate([before, keyvals, after], axis=0)
    local_lists = (neighbours - slab_index * slab_blocks + REACH) % total_blocks
    list_counts = lookup_counts(neighbours, counts)

    pairs = slab_rows * NEIGH * BLOCK * own_heads
    attended, grad_q, grad_kv = pl.pallas_call(
        functools.partial(attention_kernel, own_heads),
        grid_spec=pltpu.PrefetchScalarGridSpec(
            num_scalar_prefetch=2,
            grid=(slab_blocks,),
            in_specs=[
                pl.BlockSpec((1, BLOCK, 4 * width), lambda b, *_: (b, 0, 0)),
                pl.BlockSpec((ext_blocks, BLOCK, 2 * width), lambda b, *_: (0, 0, 0)),
            ],
            out_specs=[
                pl.BlockSpec((1, BLOCK, width), lambda b, *_: (b, 0, 0)),
                pl.BlockSpec((1, BLOCK, width), lambda b, *_: (b, 0, 0)),
                pl.BlockSpec((ext_blocks, BLOCK, 2 * width), lambda b, *_: (0, 0, 0)),
            ],
            scratch_shapes=[
                pltpu.VMEM((NEIGH, BLOCK, own_heads * BLOCK), jnp.float32),
                pltpu.VMEM((NEIGH * BLOCK, own_heads * BLOCK), bf16),
                pltpu.VMEM((NEIGH * BLOCK, own_heads * BLOCK), bf16),
            ],
        ),
        out_shape=[
            jax.ShapeDtypeStruct((slab_blocks, BLOCK, width), bf16),
            jax.ShapeDtypeStruct((slab_blocks, BLOCK, width), bf16),
            jax.ShapeDtypeStruct((ext_blocks, BLOCK, 2 * width), jnp.float32),
        ],
        compiler_params=pltpu.CompilerParams(vmem_limit_bytes=VMEM_BYTES),
        cost_estimate=pl.CostEstimate(
            flops=12 * pairs * head_dim, bytes_accessed=16 * 1024 * 1024, transcendentals=pairs
        ),
    )(local_lists.reshape(-1), list_counts.reshape(-1), own, kv_ext)

    from_next = from_behind(grad_kv[:REACH].astype(bf16), "slab", -1).astype(jnp.float32)
    from_prev = from_behind(grad_kv[REACH + slab_blocks :].astype(bf16), "slab", 1).astype(
        jnp.float32
    )
    att_dq = jnp.concatenate(
        [attended.reshape(n_head, row_count, width), grad_q.reshape(n_head, row_count, width)],
        axis=2,
    )
    att_dq = lax.all_to_all(att_dq, "head", split_axis=0, concat_axis=0, tiled=True)
    attn_rows = jnp.transpose(att_dq[:, :, :width], (1, 0, 2)).reshape(row_count, model_width)

    layer_out = jnp.dot(attn_rows, w_out, preferred_element_type=jnp.float32)
    layer_out = jnp.where(row_valid, layer_out, jnp.zeros_like(layer_out)).astype(bf16)
    term = dot(attn_rows, masked_grad, ((0,), (0,))) / math.sqrt(total_atoms)
    term = term.astype(bf16).reshape(n_head, model_width // n_head, n_slab, model_width // n_slab)
    term = jnp.transpose(term, (2, 0, 1, 3)).reshape(
        n_slab * n_head, model_width // n_head, model_width // n_slab
    )
    term = lax.all_to_all(term, ("slab", "head"), split_axis=0, concat_axis=0, tiled=True)
    grad_wo = jnp.sum(term.astype(jnp.float32), axis=0)

    own_grad = grad_kv[REACH : REACH + slab_blocks]
    own_grad = own_grad.at[slab_blocks - REACH :].add(from_next)
    own_grad = own_grad.at[:REACH].add(from_prev)
    own_grad = own_grad.astype(bf16).reshape(n_head, row_count, 2 * width)
    grad_kv_rows = lax.all_to_all(own_grad, "head", split_axis=0, concat_axis=0, tiled=True)
    grad_x = jnp.einsum(
        "grc,gmc->rm", att_dq[:, :, width:], w_groups[:, :, :width],
        preferred_element_type=jnp.float32,
    ) + jnp.einsum(
        "grc,gmc->rm", grad_kv_rows, w_groups[:, :, width:], preferred_element_type=jnp.float32
    )
    return (layer_out, grad_x.astype(bf16), grad_wo)


def solution(mesh):
    placed = (
        P(("rep", "slab", "head"), None),
        P(),
        P(),
        P(("rep", "slab"), None),
        P("rep"),
        P(("rep", "slab", "head"), None),
    )
    return jax.shard_map(
        on_device,
        mesh=mesh,
        in_specs=placed,
        out_specs=(
            P(("rep", "slab", "head"), None),
            P(("rep", "slab", "head"), None),
            P(("rep", "head"), "slab"),
        ),
        check_vma=False,
    )
```

time: 749 us -> 385 us (0.51)
  local copies, waits for them, and re-layouts: 201 us -> 20 us
  matrix products: 175 us -> 13.4 us
  other arithmetic: 130 us -> 18.4 us
  Pallas kernels: 0 us -> 104 us
  blocking collectives: 0 us -> 99.5 us
  waiting for transfers between devices: 204 us -> 111 us
  between operations: 14 us -> 0.8 us
    dot_general x61 -> x4, matrix products: 175 us -> 13.4 us  [the longest x1 4.47 us: on_device(): jnp.einsum('grc,gmc->rm', grad_kv_rows, w_groups[:, :, width:], preferred...]
    pallas_call x0 -> x2, Pallas kernels: none -> 104 us  [the longest x1 99.3 us: on_device(): pl.pallas_call(functools.partial(attention_kernel, own_heads), grid_spec=...]
    all_to_all x0 -> x1, blocking collectives: none -> 99.5 us  [on_device(): lax.all_to_all(projected, 'head', split_axis=0, concat_axis=0, tiled=True)]
    all_gather x1 -> x0, waiting for transfers between devices: 93.8 us -> none  [on_device(): lax.all_gather(atom_feats, 'head', axis=0, tiled=True)]
    all_to_all x3, waiting for transfers between devices: 5.27 us -> 91.2 us  [the longest x1 42.1 us: on_device(): lax.all_to_all(att_dq, 'head', split_axis=0, concat_axis=0, tiled=True)]
    scatter-add x8 -> x0, other arithmetic: 80.5 us -> none  [backward_group(): carry = carry.at[lists.reshape(-1)].add(both)]
    gather x16 -> x0, local copies, waits for them, and re-layouts: 69.3 us -> none  [gather_keys(): picked = kv_ext[lists]]
    unnamed x4 -> x0, waiting for transfers between devices: 59 us -> none
  transfers between devices with their start and end apart: 10 -> 7, of which waited for: 7 -> 5; matrix products, arithmetic and copies ran while one was open for 10% -> 8% of each run, Pallas kernels for 0% -> 0%
where the time goes in v1:
time: 385 us; the launch traced here: 384 us
  waiting for transfers between devices  111 us (29%)
  Pallas kernels  104 us (27%)
  blocking collectives  99.5 us (26%)
  local copies, waits for them, and re-layouts  20 us (5%)
  other arithmetic  18.4 us (5%)
  starting transfers between devices  16.4 us (4%)
  matrix products  13.4 us (3%)
    all_to_all x1, blocking collectives, on_device(): lax.all_to_all(projected, 'head', split_axis=0, concat_axis=0, tiled=True)  99.5 us
    pallas_call x1, Pallas kernels, on_device(): pl.pallas_call(functools.partial(attention_kernel, own_heads), grid_spec=...  99.3 us
    all_to_all x1, waiting for transfers between devices, on_device(): lax.all_to_all(att_dq, 'head', split_axis=0, concat_axis=0, tiled=True)  42.1 us
    all_to_all x1, waiting for transfers between devices, on_device(): lax.all_to_all(own_grad, 'head', split_axis=0, concat_axis=0, tiled=True)  41.5 us
    ppermute x4, waiting for transfers between devices, from_behind(): lax.ppermute(shard, axis, [(i, (i + by) % count) for i in range(count)])  20.3 us
  transfers between devices with their start and end apart: 7, of which 5 were waited for; matrix products, arithmetic and copies ran while one was open for 8% of the time, Pallas kernels for 0%

profile of v1, /device:TPU:0, one launch (start us, length us, event | category | flops | bytes accessed | tf_op | source)
XLA Modules:
  0.0 384.1 jit_solution(16195546280113047532)
XLA Ops:
  0.7 1.0 select_reduce_fusion
  1.7 2.7 copy.28
  4.4 0.0 copy-start.1
  4.4 1.9 copy.29.w_ref
  6.4 0.0 copy-start
  6.4 1.5 broadcast_select_fusion.g_ref
  7.9 0.0 copy-done.1
  7.9 0.0 copy-done
  7.9 5.0 %shard_map.85 = bf16[4,1024,512]{2,1,0:T(8,128)(2,1)} custom-call(bf16[1024,512]{1,0:T(8,128)(2,1)S(1)} %copy-done, bf16[1024,512]{1,0:T(8,128)(2,1)S(1)} %broadcast_select_fusion.g_ref, bf16[4,512,384]{2,1,0:T(8,128)(2,1)S(1)} %copy.29.w_ref, bf16[512,512]{1,0:T(8,128)(2,1)S(1)} %copy-done.1), custom_call_target="tpu_custom_call" | custom-call | tf_op jit(solution)/shard_map/pallas_call | solution.py:140
  12.9 99.5 %all_to_all.20 = bf16[4,1024,512]{2,1,0:T(8,128)(2,1)S(1)} all-to-all(bf16[4,1024,512]{2,1,0:T(8,128)(2,1)} %shard_map.85), channel_id=1, replica_groups=mesh['rep'=2,'slab'=4,'head'=4] {'head'}, dimensions={0} | all-to-all | bytes 8388608 | tf_op jit(solution)/shard_map/all_to_all | solution.py:153
  112.4 0.0 copy-start.2
  112.4 0.0 copy-start.3
  112.4 0.0 copy-start.4
  112.4 1.6 fusion.15
  114.0 1.0 copy-done.2
  115.0 0.0 collective-permute-start
  115.1 1.7 collective-permute-start.1
  116.8 0.0 copy-done.3
  116.8 0.1 copy.27
  116.9 0.1 copy.26
  117.0 0.1 reshape.135.lists
  117.1 0.0 copy-done.4
  117.1 0.7 select_reduce_fusion.1
  117.7 0.1 reshape.136.list_counts
  117.8 1.7 slice.96
  119.6 19.4 %collective-permute-done = bf16[16,128,256]{2,1,0:T(8,128)(2,1)} collective-permute-done((bf16[16,128,256]{2,1,0:T(8,128)(2,1)}, bf16[16,128,256]{2,1,0:T(8,128)(2,1)}, u32[]{:S(2)}, u32[]{:S(2)}) %collective-permute-start) | collective-permute-done | bytes 1048608 | tf_op jit(solution)/shard_map/ppermute | solution.py:19
  139.0 0.9 collective-permute-done.1
  139.8 3.4 pad_maximum_fusion.kv_ref
  143.2 99.3 %shard_map.86 = (bf16[32,128,128]{2,1,0:T(8,128)(2,1)S(1)}, bf16[32,128,128]{2,1,0:T(8,128)(2,1)S(1)}, f32[64,128,256]{2,1,0:T(8,128)}) custom-call(s32[256]{0:T(256)S(1)} %reshape.135.lists, s32[256]{0:T(256)S(1)} %reshape.136.list_counts, bf16[32,128,512]{2,1,0:T(8,128)(2,1)} %bitcast.29, bf16[64,128,256]{2,1,0:T(8,128)(2,1)} %pad_maximum_fusion.kv_ref), custom_call_target="tpu_custom_call" | custom-call | flops 6442450944 | bytes 16777216 | tf_op jit(solution)/shard_map/pallas_call | solution.py:164
  242.5 1.6 pad_maximum_fusion.1
  244.0 4.5 %all-to-all-start.1 = ((bf16[4,1024,256]{2,1,0:T(8,128)(2,1)}), bf16[4,1024,256]{2,1,0:T(8,128)(2,1)}, u32[]{:S(2)}, u32[]{:S(2)}) async-start(bf16[4,1024,256]{2,1,0:T(8,128)(2,1)} %pad_maximum_fusion.1), calls=%async_computation.1 | async-start | bytes 4194304 | tf_op jit(solution)/shard_map/all_to_all | solution.py:203
  248.5 4.0 %convert.4 = bf16[64,128,256]{2,1,0:T(8,128)(2,1)S(1)} convert(f32[64,128,256]{2,1,0:T(8,128)} %get-tuple-element.32) | non-fusion elementwise | flops 2097152 | bytes 12582912 | tf_op jit(solution)/shard_map/convert.1
  252.5 1.5 fusion.14
  254.0 1.9 collective-permute-start.2
  255.9 0.0 collective-permute-start.3
  255.9 42.1 %all-to-all-done.1 = bf16[4,1024,256]{2,1,0:T(8,128)(2,1)} async-done(((bf16[4,1024,256]{2,1,0:T(8,128)(2,1)}), bf16[4,1024,256]{2,1,0:T(8,128)(2,1)}, u32[]{:S(2)}, u32[]{:S(2)}) %all-to-all-start.1) | async-done | bytes 2097184 | tf_op jit(solution)/shard_map/all_to_all | solution.py:203
  298.0 2.3 slice_bitcast_fusion
  300.3 2.2 copy.30
  302.6 2.7 fusion.2
  305.3 1.2 reshape.144
  306.4 0.9 copy.33
  307.3 3.8 all-to-all-start.3
  311.1 2.5 slice.89
  313.7 0.0 collective-permute-done.2
  313.7 2.2 add_dynamic-update-slice_fusion
  315.9 0.0 collective-permute-done.3
  315.9 1.7 fusion
  317.6 1.6 convert_element_type.26
  319.2 7.6 %all-to-all-done.3 = bf16[16,128,128]{2,1,0:T(8,128)(2,1)S(1)} async-done(((bf16[16,128,128]{2,1,0:T(8,128)(2,1)}), bf16[16,128,128]{2,1,0:T(8,128)(2,1)S(1)}, u32[]{:S(2)}, u32[]{:S(2)}) %all-to-all-start.3) | async-done | bytes 524320 | tf_op jit(solution)/shard_map/all_to_all | solution.py:213
  326.8 4.4 %all-to-all-start.2 = ((bf16[4,1024,256]{2,1,0:T(8,128)(2,1)}), bf16[4,1024,256]{2,1,0:T(8,128)(2,1)}, u32[]{:S(2)}, u32[]{:S(2)}) async-start(bf16[4,1024,256]{2,1,0:T(8,128)(2,1)} %bitcast.30), calls=%async_computation.2 | async-start | bytes 4194304 | tf_op jit(solution)/shard_map/all_to_all | solution.py:220
  331.3 3.0 select_convert_fusion
  334.2 3.3 fusion.4
  337.5 0.7 convert_reduce_fusion
  338.2 41.5 %all-to-all-done.2 = bf16[4,1024,256]{2,1,0:T(8,128)(2,1)} async-done(((bf16[4,1024,256]{2,1,0:T(8,128)(2,1)}), bf16[4,1024,256]{2,1,0:T(8,128)(2,1)}, u32[]{:S(2)}, u32[]{:S(2)}) %all-to-all-start.2) | async-done | bytes 2097184 | tf_op jit(solution)/shard_map/all_to_all | solution.py:220
  379.7 4.5 %fusion.1 = bf16[1024,512]{1,0:T(8,128)(2,1)} fusion(f32[1024,512,1]{1,0,2:T(8,128)} %fusion.4, bf16[4,1024,256]{2,1,0:T(8,128)(2,1)} %all-to-all-done.2, bf16[4,512,384]{2,1,0:T(8,128)(2,1)S(1)} %copy.29.w_ref), kind=kOutput, calls=%fused_computation.5 | convolution fusion | flops 1074790400 | bytes 6291456 | tf_op jit(solution)/shard_map/grc,gmc->rm/dot_general | solution.py:224
  (3 shorter events, 0.0 us)
Async XLA Ops:
  4.4 3.5 copy-start.1
  6.4 1.5 copy-start
  112.4 2.7 copy-start.2
  112.4 4.4 %copy-start.3 = (s32[32,8]{0,1:T(8,128)S(1)}, s32[32,8]{0,1:T(8,128)}, u32[]{:S(2)}) copy-start(s32[32,8]{0,1:T(8,128)} %param.13) | copy-start | bytes 3076
  112.4 4.7 %copy-start.4 = (s32[128]{0:T(128)S(1)}, s32[128]{0:T(128)}, u32[]{:S(2)}) copy-start(s32[128]{0:T(128)} %param.14) | copy-start | bytes 1540
  115.0 23.9 %collective-permute-start = (bf16[16,128,256]{2,1,0:T(8,128)(2,1)}, bf16[16,128,256]{2,1,0:T(8,128)(2,1)}, u32[]{:S(2)}, u32[]{:S(2)}) collective-permute-start(bf16[16,128,256]{2,1,0:T(8,128)(2,1)} %get-tuple-element.35), channel_id=1, source_target_pairs={{0,4},{4,8},{8,12},{12,0},{1,5},{5,9},{9,13},{13,1},{2,6},{6,10},{... | collective-permute-start | bytes 3145736 | tf_op jit(solution)/shard_map/ppermute | solution.py:19
  115.1 24.8 %collective-permute-start.1 = (bf16[16,128,256]{2,1,0:T(8,128)(2,1)}, bf16[16,128,256]{2,1,0:T(8,128)(2,1)}, u32[]{:S(2)}, u32[]{:S(2)}) collective-permute-start(bf16[16,128,256]{2,1,0:T(8,128)(2,1)} %get-tuple-element.36), channel_id=1, source_target_pairs={{0,12},{4,0},{8,4},{12,8},{1,13},{5,1},{9,5},{13,9},{2,14},{6,2},{... | collective-permute-start | bytes 3145736 | tf_op jit(solution)/shard_map/ppermute | solution.py:19
  244.0 54.0 %all-to-all-start.1 = ((bf16[4,1024,256]{2,1,0:T(8,128)(2,1)}), bf16[4,1024,256]{2,1,0:T(8,128)(2,1)}, u32[]{:S(2)}, u32[]{:S(2)}) async-start(bf16[4,1024,256]{2,1,0:T(8,128)(2,1)} %pad_maximum_fusion.1), calls=%async_computation.1 | async-start | bytes 4194304 | tf_op jit(solution)/shard_map/all_to_all | solution.py:203
  254.0 59.7 %collective-permute-start.2 = (bf16[16,128,256]{2,1,0:T(8,128)(2,1)}, bf16[16,128,256]{2,1,0:T(8,128)(2,1)}, u32[]{:S(2)}, u32[]{:S(2)}) collective-permute-start(bf16[16,128,256]{2,1,0:T(8,128)(2,1)} %get-tuple-element.34), channel_id=1, source_target_pairs={{0,12},{4,0},{8,4},{12,8},{1,13},{5,1},{9,5},{13,9},{2,14},{6,2},{... | collective-permute-start | bytes 3145736 | tf_op jit(solution)/shard_map/ppermute | solution.py:19
  255.9 60.0 %collective-permute-start.3 = (bf16[16,128,256]{2,1,0:T(8,128)(2,1)}, bf16[16,128,256]{2,1,0:T(8,128)(2,1)}, u32[]{:S(2)}, u32[]{:S(2)}) collective-permute-start(bf16[16,128,256]{2,1,0:T(8,128)(2,1)} %get-tuple-element.33), channel_id=1, source_target_pairs={{0,4},{4,8},{8,12},{12,0},{1,5},{5,9},{9,13},{13,1},{2,6},{6,10},{... | collective-permute-start | bytes 3145736 | tf_op jit(solution)/shard_map/ppermute | solution.py:19
  307.3 19.5 %all-to-all-start.3 = ((bf16[16,128,128]{2,1,0:T(8,128)(2,1)}), bf16[16,128,128]{2,1,0:T(8,128)(2,1)S(1)}, u32[]{:S(2)}, u32[]{:S(2)}) async-start(bf16[16,128,128]{2,1,0:T(8,128)(2,1)} %bitcast.12), calls=%async_computation.3 | async-start | bytes 1048576 | tf_op jit(solution)/shard_map/all_to_all | solution.py:213
  326.8 52.8 %all-to-all-start.2 = ((bf16[4,1024,256]{2,1,0:T(8,128)(2,1)}), bf16[4,1024,256]{2,1,0:T(8,128)(2,1)}, u32[]{:S(2)}, u32[]{:S(2)}) async-start(bf16[4,1024,256]{2,1,0:T(8,128)(2,1)} %bitcast.30), calls=%async_computation.2 | async-start | bytes 4194304 | tf_op jit(solution)/shard_map/all_to_all | solution.py:220

commit v2 on v1

v2 whole, which is shorter than its diff:
```python
import functools
import math

import jax
import jax.numpy as jnp
from jax import lax
from jax.experimental import pallas as pl
from jax.experimental.pallas import tpu as pltpu
from jax.sharding import PartitionSpec as P

BLOCK = 128
NEIGH = 8
REACH = 16
TOGETHER = 2
VMEM_BYTES = 48 * 1024 * 1024


def from_behind(shard, axis, by):
    count = lax.axis_size(axis)
    return lax.ppermute(shard, axis, [(i, (i + by) % count) for i in range(count)])


def lookup_counts(block_ids, counts):
    table_ids = jnp.arange(counts.shape[0], dtype=jnp.int32)
    hits = block_ids[..., None] == table_ids
    return jnp.sum(jnp.where(hits, counts, 0), axis=-1)


def dot(a, b, dims):
    return lax.dot_general(a, b, (dims, ((), ())), preferred_element_type=jnp.float32)


def project_kernel(parts, x_ref, g_ref, w_ref, wo_ref, *out_refs):
    width = wo_ref.shape[0] // parts
    qkv = dot(x_ref[...], w_ref[0], ((1,), (0,))).astype(jnp.bfloat16)
    d_attn = dot(g_ref[...], wo_ref[...], ((1,), (1,))).astype(jnp.bfloat16)
    for part, out_ref in enumerate(out_refs):
        columns = slice(part * width, (part + 1) * width)
        wide = slice(part * 3 * width, (part + 1) * 3 * width)
        out_ref[0] = jnp.concatenate([qkv[:, wide], d_attn[:, columns]], axis=1)


def attention_kernel(
    heads, lists, list_counts, own_ref, kv_ref, out_ref, dkv_ref,
    turned_ref, l_ref, lt_ref, s_ref, p_ref, g_ref, sum_ref,
):
    step = pl.program_id(0)
    together = own_ref.shape[0]
    ext_blocks = kv_ref.shape[0]
    width = out_ref.shape[2] // 2
    head_dim = width // heads
    lanes = heads * BLOCK
    scale = 1.0 / math.sqrt(head_dim)
    exp_scale = scale * math.log2(math.e)
    each = range(together)
    bf16 = jnp.bfloat16

    @pl.when(step == 0)
    def _():
        dkv_ref[...] = jnp.zeros_like(dkv_ref)

        @pl.loop(0, ext_blocks)
        def _(block):
            turned_ref[block] = kv_ref[block].T

    row_head = lax.broadcasted_iota(jnp.int32, (2 * width, lanes), 0) // head_dim
    lane_head = lax.broadcasted_iota(jnp.int32, (2 * width, lanes), 1) // BLOCK
    column = lax.broadcasted_iota(jnp.int32, (1, 2 * width), 1)
    column_scale = jnp.where(column < width, scale, 1.0)
    slots = lax.broadcasted_iota(jnp.int32, (BLOCK, 1), 0)
    first = step * (together * NEIGH)
    ids = [[lists[first + u * NEIGH + n] for n in range(NEIGH)] for u in each]
    spans = [slice(n * BLOCK, (n + 1) * BLOCK) for n in range(NEIGH)]

    def valid(u, n):
        return slots < list_counts[first + u * NEIGH + n]

    def pick_diagonal(full):
        return [
            full[h * head_dim : (h + 1) * head_dim, h * BLOCK : (h + 1) * BLOCK]
            for h in range(heads)
        ]

    q_bd, grad_bd = [], []
    for u in each:
        for n in range(NEIGH):
            l_ref[u, spans[n]] = kv_ref[ids[u][n]]
            lt_ref[u, :, spans[n]] = turned_ref[ids[u][n]]
        turned = own_ref[u, :, 2 * width :].astype(jnp.float32).T
        turned = jnp.concatenate([turned] * heads, axis=1)
        q_bd.append(jnp.where(row_head == lane_head, turned, 0.0).astype(bf16))
        grad_bd.append(jnp.where(row_head - heads == lane_head, turned, 0.0))
    for u in each:
        s_ref[u] = dot(l_ref[u], q_bd[u], ((1,), (0,)))

    inverse = []
    for u in each:
        top = jnp.full((8, lanes), -jnp.inf, jnp.float32)
        for n in range(NEIGH):
            scores = jnp.where(valid(u, n), s_ref[u, spans[n]], -jnp.inf)
            top = jnp.maximum(top, jnp.max(scores.reshape(BLOCK // 8, 8, lanes), axis=0))
        top = jnp.max(top, axis=0, keepdims=True) * exp_scale
        total = jnp.zeros((8, lanes), jnp.float32)
        for n in range(NEIGH):
            p = jnp.where(valid(u, n), jnp.exp2(s_ref[u, spans[n]] * exp_scale - top), 0.0)
            total += jnp.sum(p.reshape(BLOCK // 8, 8, lanes), axis=0)
            p_ref[u, spans[n]] = p.astype(bf16)
        inverse.append(1.0 / jnp.sum(total, axis=0, keepdims=True))

    delta, attended, right = [], [], []
    for u in each:
        att_full = dot(lt_ref[u, width:], p_ref[u], ((1,), (0,))) * inverse[u]
        attended.append(att_full)
        att_round = att_full.astype(bf16).astype(jnp.float32)
        rounded = (grad_bd[u] * inverse[u]).astype(bf16)
        grad_bd[u] = rounded
        delta.append(
            jnp.sum(rounded[width:].astype(jnp.float32) * att_round, axis=0, keepdims=True)
        )
        right.append(jnp.concatenate([q_bd[u].T, rounded.T], axis=0))
    for u in each:
        s_ref[u] = dot(l_ref[u], grad_bd[u], ((1,), (0,)))
    for u in each:
        for n in range(NEIGH):
            p = p_ref[u, spans[n]].astype(jnp.float32)
            g_ref[u, spans[n]] = (p * (s_ref[u, spans[n]] - delta[u])).astype(bf16)
    for u in each:
        both = jnp.concatenate([g_ref[u], p_ref[u]], axis=1)
        sum_ref[u] = dot(both, right[u], ((1,), (0,))) * column_scale
    for u in each:
        dq_full = dot(lt_ref[u, :width], g_ref[u], ((1,), (0,))) * scale
        rows = pick_diagonal(attended[u]) + pick_diagonal(dq_full)
        out_ref[u] = jnp.concatenate(rows, axis=0).T.astype(bf16)
    for u in each:
        for n in range(NEIGH):
            dkv_ref[ids[u][n]] += sum_ref[u, spans[n]]


def exchange(blocks):
    return lax.all_to_all(blocks, "head", split_axis=0, concat_axis=0, tiled=True)


def after_of(value, earlier):
    return lax.optimization_barrier((value, earlier))[0]


def on_device(atom_feats, w_qkv, w_out, neighbours, counts, d_out):
    row_count, model_width = atom_feats.shape
    n_head = lax.axis_size("head")
    n_slab = lax.axis_size("slab")
    heads_all = w_qkv.shape[1]
    head_dim = w_qkv.shape[2] // 3
    own_heads = heads_all // n_head
    slab_blocks = neighbours.shape[0]
    slab_rows = row_count * n_head
    total_blocks = slab_blocks * n_slab
    total_atoms = slab_rows * n_slab
    ext_blocks = slab_blocks + 2 * REACH
    list_rows = NEIGH * BLOCK
    head_index = lax.axis_index("head")
    slab_index = lax.axis_index("slab")
    bf16 = jnp.bfloat16

    row_global = (slab_index * n_head + head_index) * row_count + jnp.arange(
        row_count, dtype=jnp.int32
    )
    row_counts = lookup_counts(row_global // BLOCK, counts)
    row_valid = (row_global % BLOCK < row_counts)[:, None]
    masked_grad = jnp.where(row_valid, d_out, jnp.zeros_like(d_out))
    parts = 2 if own_heads % 2 == 0 else 1
    heads = own_heads // parts
    width = heads * head_dim
    w_groups = w_qkv.reshape(model_width, n_head, parts, heads, 3, head_dim)
    w_groups = jnp.transpose(
        jnp.stack([w_groups[..., t, :] for t in (1, 2, 0)], axis=4), (1, 0, 2, 4, 3, 5)
    ).reshape(n_head, model_width, parts * 3 * width)

    projected = pl.pallas_call(
        functools.partial(project_kernel, parts),
        grid=(n_head,),
        in_specs=[
            pl.BlockSpec((row_count, model_width), lambda g: (0, 0)),
            pl.BlockSpec((row_count, model_width), lambda g: (0, 0)),
            pl.BlockSpec((1, model_width, parts * 3 * width), lambda g: (g, 0, 0)),
            pl.BlockSpec((parts * width, model_width), lambda g: (g, 0)),
        ],
        out_specs=[pl.BlockSpec((1, row_count, 4 * width), lambda g: (g, 0, 0))] * parts,
        out_shape=[jax.ShapeDtypeStruct((n_head, row_count, 4 * width), bf16)] * parts,
        compiler_params=pltpu.CompilerParams(vmem_limit_bytes=VMEM_BYTES),
    )(atom_feats, masked_grad, w_groups, w_out)
    local_lists = (neighbours - slab_index * slab_blocks + REACH) % total_blocks
    local_lists = local_lists.reshape(-1)
    list_counts = lookup_counts(neighbours, counts).reshape(-1)
    pairs = slab_rows * NEIGH * BLOCK * heads

    def attend(own, before, after):
        kv_ext = jnp.concatenate([before, own[:, :, : 2 * width], after], axis=0)
        return pl.pallas_call(
            functools.partial(attention_kernel, heads),
            grid_spec=pltpu.PrefetchScalarGridSpec(
                num_scalar_prefetch=2,
                grid=(slab_blocks // TOGETHER,),
                in_specs=[
                    pl.BlockSpec((TOGETHER, BLOCK, 4 * width), lambda b, *_: (b, 0, 0)),
                    pl.BlockSpec((ext_blocks, BLOCK, 2 * width), lambda b, *_: (0, 0, 0)),
                ],
                out_specs=[
                    pl.BlockSpec((TOGETHER, BLOCK, 2 * width), lambda b, *_: (b, 0, 0)),
                    pl.BlockSpec((ext_blocks, BLOCK, 2 * width), lambda b, *_: (0, 0, 0)),
                ],
                scratch_shapes=[
                    pltpu.VMEM((ext_blocks, 2 * width, BLOCK), bf16),
                    pltpu.VMEM((TOGETHER, list_rows, 2 * width), bf16),
                    pltpu.VMEM((TOGETHER, 2 * width, list_rows), bf16),
                    pltpu.VMEM((TOGETHER, list_rows, heads * BLOCK), jnp.float32),
                    pltpu.VMEM((TOGETHER, list_rows, heads * BLOCK), bf16),
                    pltpu.VMEM((TOGETHER, list_rows, heads * BLOCK), bf16),
                    pltpu.VMEM((TOGETHER, list_rows, 2 * width), jnp.float32),
                ],
            ),
            out_shape=[
                jax.ShapeDtypeStruct((slab_blocks, BLOCK, 2 * width), bf16),
                jax.ShapeDtypeStruct((ext_blocks, BLOCK, 2 * width), jnp.float32),
            ],
            compiler_params=pltpu.CompilerParams(vmem_limit_bytes=VMEM_BYTES),
            cost_estimate=pl.CostEstimate(
                flops=400 * pairs * head_dim, bytes_accessed=8 << 20, transcendentals=pairs
            ),
        )(local_lists, list_counts, own, kv_ext)

    received, results = [], []
    for part in range(parts):
        blocks = projected[part]
        if part:
            blocks = after_of(blocks, received[-1])
        received.append(exchange(blocks).reshape(slab_blocks, BLOCK, 4 * width))
    for part in range(parts):
        own = received[part]
        keyvals = own[:, :, : 2 * width]
        before = from_behind(keyvals[slab_blocks - REACH :], "slab", 1)
        after = from_behind(keyvals[:REACH], "slab", -1)
        results.append(attend(own, before, after))

    att_dq, grad_kv_rows = [], []
    for rows, grad_kv in results:
        from_next = from_behind(grad_kv[:REACH].astype(bf16), "slab", -1)
        from_prev = from_behind(grad_kv[REACH + slab_blocks :].astype(bf16), "slab", 1)
        att_dq.append(exchange(rows.reshape(n_head, row_count, 2 * width)))
        own_grad = grad_kv[REACH : REACH + slab_blocks]
        own_grad = own_grad.at[slab_blocks - REACH :].add(from_next.astype(jnp.float32))
        own_grad = own_grad.at[:REACH].add(from_prev.astype(jnp.float32))
        own_grad = own_grad.astype(bf16).reshape(n_head, row_count, 2 * width)
        grad_kv_rows.append(exchange(own_grad))

    attn_rows = jnp.stack([rows[:, :, :width] for rows in att_dq], axis=1)
    attn_rows = jnp.transpose(attn_rows, (2, 0, 1, 3)).reshape(row_count, model_width)
    layer_out = jnp.dot(attn_rows, w_out, preferred_element_type=jnp.float32)
    layer_out = jnp.where(row_valid, layer_out, jnp.zeros_like(layer_out)).astype(bf16)
    term = dot(attn_rows, masked_grad, ((0,), (0,))) / math.sqrt(total_atoms)
    term = term.astype(bf16).reshape(n_head, model_width // n_head, n_slab, model_width // n_slab)
    term = jnp.transpose(term, (2, 0, 1, 3)).reshape(
        n_slab * n_head, model_width // n_head, model_width // n_slab
    )
    term = lax.all_to_all(term, ("slab", "head"), split_axis=0, concat_axis=0, tiled=True)
    grad_wo = jnp.sum(term.astype(jnp.float32), axis=0)

    grad_x = jnp.zeros((row_count, model_width), jnp.float32)
    for part in range(parts):
        columns = [grad_kv_rows[part], att_dq[part][:, :, width:]]
        columns = jnp.concatenate(columns, axis=2)
        weights = w_groups[:, :, part * 3 * width : (part + 1) * 3 * width]
        grad_x += jnp.einsum("grc,gmc->rm", columns, weights, preferred_element_type=jnp.float32)
    return (layer_out, grad_x.astype(bf16), grad_wo)


def solution(mesh):
    placed = (
        P(("rep", "slab", "head"), None),
        P(),
        P(),
        P(("rep", "slab"), None),
        P("rep"),
        P(("rep", "slab", "head"), None),
    )
    return jax.shard_map(
        on_device,
        mesh=mesh,
        in_specs=placed,
        out_specs=(
            P(("rep", "slab", "head"), None),
            P(("rep", "slab", "head"), None),
            P(("rep", "head"), "slab"),
        ),
        check_vma=False,
    )
```

time: 385 us -> 309 us (0.80)
  blocking collectives: 99.5 us -> 54.5 us
  waiting for transfers between devices: 111 us -> 71.6 us
  starting transfers between devices: 16.4 us -> 32 us
  matrix products: 13.4 us -> 7.72 us
  other arithmetic: 18.4 us -> 14.1 us
    all_to_all x2 -> x5, waiting for transfers between devices: 83.6 us -> 22.6 us  [exchange(): lax.all_to_all(blocks, 'head', split_axis=0, concat_axis=0, tiled=True)]
    all_to_all x1, blocking collectives: 99.5 us -> 54.5 us  [exchange(): lax.all_to_all(blocks, 'head', split_axis=0, concat_axis=0, tiled=True)]
    ppermute x4 -> x8, waiting for transfers between devices: 20.3 us -> 39.7 us  [from_behind(): lax.ppermute(shard, axis, [(i, (i + by) % count) for i in range(count)])]
    all_to_all x2 -> x5, starting transfers between devices: 8.94 us -> 21.3 us  [exchange(): lax.all_to_all(blocks, 'head', split_axis=0, concat_axis=0, tiled=True)]
    transpose x3 -> x2, local copies, waits for them, and re-layouts: 7.24 us -> 1.34 us  [the longest x1 1.27 us: on_device(): jnp.transpose(jnp.stack([w_groups[..., t, :] for t in (1, 2, 0)], axis=4)...]
    reshape x3 -> x7, local copies, waits for them, and re-layouts: 2.13 us -> 7.42 us  [the longest x2 2.63 us: on_device(): own_grad = own_grad.astype(bf16).reshape(n_head, row_count, 2 * width)]
    slice x1 -> x6, local copies, waits for them, and re-layouts: 1.73 us -> 5.77 us  [the longest x2 2.99 us: on_device(): columns = [grad_kv_rows[part], att_dq[part][:, :, width:]]]
    pallas_call x2 -> x3, Pallas kernels: 104 us -> 104 us  [the longest x2 98.4 us: attend(): pl.pallas_call(functools.partial(attention_kernel, heads), grid_spec=pltp...]
  transfers between devices with their start and end apart: 7 -> 14, of which waited for: 5 -> 10; matrix products, arithmetic and copies ran while one was open for 8% -> 10% of each run, Pallas kernels for 0% -> 32%
where the time goes in v2:
time: 309 us; the launch traced here: 308 us
  Pallas kernels  104 us (34%)
  waiting for transfers between devices  71.6 us (23%)
  blocking collectives  54.5 us (18%)
  starting transfers between devices  32 us (10%)
  local copies, waits for them, and re-layouts  23.1 us (7%)
  other arithmetic  14.1 us (5%)
  matrix products  7.72 us (2%)
    pallas_call x2, Pallas kernels, attend(): pl.pallas_call(functools.partial(attention_kernel, heads), grid_spec=pltp...  98.4 us
    all_to_all x1, blocking collectives, exchange(): lax.all_to_all(blocks, 'head', split_axis=0, concat_axis=0, tiled=True)  54.5 us
    ppermute x8, waiting for transfers between devices, from_behind(): lax.ppermute(shard, axis, [(i, (i + by) % count) for i in range(count)])  39.7 us
    all_to_all x5, waiting for transfers between devices, exchange(): lax.all_to_all(blocks, 'head', split_axis=0, concat_axis=0, tiled=True)  22.6 us
    all_to_all x5, starting transfers between devices, exchange(): lax.all_to_all(blocks, 'head', split_axis=0, concat_axis=0, tiled=True)  21.3 us
    all_to_all x1, waiting for transfers between devices, on_device(): lax.all_to_all(term, ('slab', 'head'), split_axis=0, concat_axis=0, tiled...  9.38 us
    ppermute x8, starting transfers between devices, from_behind(): lax.ppermute(shard, axis, [(i, (i + by) % count) for i in range(count)])  6.26 us
  transfers between devices with their start and end apart: 14, of which 10 were waited for; matrix products, arithmetic and copies ran while one was open for 10% of the time, Pallas kernels for 32%

profile of v2, /device:TPU:0, one launch (start us, length us, event | category | flops | bytes accessed | tf_op | source)
XLA Modules:
  0.0 307.8 jit_solution(2954712164663313658)
XLA Ops:
  0.6 1.3 slice.194
  2.0 1.1 slice.195
  3.1 0.4 select_reduce_fusion
  3.5 0.1 maximum_bitcast_fusion
  3.6 1.3 copy.39
  4.9 2.0 copy.40.w_ref
  6.9 1.4 broadcast_select_fusion.g_ref
  8.4 5.3 %shard_map.85 = (bf16[4,1024,256]{2,1,0:T(8,128)(2,1)}, bf16[4,1024,256]{2,1,0:T(8,128)(2,1)}) custom-call(bf16[1024,512]{1,0:T(8,128)(2,1)S(1)} %copy-done.5, bf16[1024,512]{1,0:T(8,128)(2,1)S(1)} %broadcast_select_fusion.g_ref, bf16[4,512,384]{2,1,0:T(8,128)(2,1)S(1)} %copy.40.w_ref, bf16[512,512]{1,0:T(8,128)(2,1)S(1)} %copy-done.6), custom_call_target="tpu_custom_call" | custom-call | tf_op jit(solution)/shard_map/pallas_call | solution.py:178
  13.6 54.5 %all_to_all.35 = bf16[4,1024,256]{2,1,0:T(8,128)(2,1)S(1)} all-to-all(bf16[4,1024,256]{2,1,0:T(8,128)(2,1)} %get-tuple-element.58), channel_id=1, replica_groups=mesh['rep'=2,'slab'=4,'head'=4] {'head'}, dimensions={0} | all-to-all | bytes 4194304 | tf_op jit(solution)/shard_map/all_to_all | solution.py:140
  68.2 1.4 fusion.24
  69.5 1.7 collective-permute-start.1
  71.5 0.7 select_reduce_fusion.1
  72.3 0.2 slice.197
  72.5 3.6 %all-to-all-start.2 = ((bf16[4,1024,256]{2,1,0:T(8,128)(2,1)}), bf16[4,1024,256]{2,1,0:T(8,128)(2,1)S(1)}, u32[]{:S(2)}, u32[]{:S(2)}) async-start(bf16[4,1024,256]{2,1,0:T(8,128)(2,1)} %get-tuple-element.61), calls=%async_computation.2 | async-start | bytes 4194304 | tf_op jit(solution)/shard_map/all_to_all | solution.py:140
  76.2 6.0 %collective-permute-done = bf16[16,128,128]{2,1,0:T(8,128)(2,1)} collective-permute-done((bf16[16,128,128]{2,1,0:T(8,128)(2,1)}, bf16[16,128,128]{2,1,0:T(8,128)(2,1)}, u32[]{:S(2)}, u32[]{:S(2)}) %collective-permute-start) | collective-permute-done | bytes 524320 | tf_op jit(solution)/shard_map/ppermute | solution.py:20
  82.2 0.9 collective-permute-done.1
  83.1 1.4 pad_maximum_fusion.kv_ref
  84.5 49.2 %shard_map.86 = (bf16[32,128,128]{2,1,0:T(8,128)(2,1)S(1)}, f32[64,128,128]{2,1,0:T(8,128)}) custom-call(s32[256]{0:T(256)S(1)} %reshape.197.lists, s32[256]{0:T(256)S(1)} %reshape.198.list_counts, bf16[32,128,256]{2,1,0:T(8,128)(2,1)S(1)} %bitcast.35, bf16[64,128,128]{2,1,0:T(8,128)(2,1)S(1)} %pad_maximum_fusion.kv_ref), custom_call_target="tpu_custom_call" | custom-call | flops 107374182400 | bytes 8388608 | tf_op jit(solution)/shard_map/pallas_call | solution.py:198
  133.7 1.3 copy.41
  135.0 4.3 %all-to-all-start.1 = ((bf16[4,1024,128]{1,2,0:T(8,128)(2,1)}), bf16[4,1024,128]{1,2,0:T(8,128)(2,1)}, u32[]{:S(2)}, u32[]{:S(2)}) async-start(bf16[4,1024,128]{1,2,0:T(8,128)(2,1)} %copy.41), calls=%async_computation.1 | async-start | bytes 2097152 | tf_op jit(solution)/shard_map/all_to_all | solution.py:140
  139.3 2.7 convert.8
  142.2 2.2 collective-permute-start.4
  144.3 0.2 slice.180
  144.6 1.2 fusion.25
  145.8 0.6 collective-permute-start.2
  146.4 1.1 collective-permute-start.3
  147.5 8.9 %collective-permute-done.4 = bf16[16,128,128]{2,1,0:T(8,128)(2,1)S(1)} collective-permute-done((bf16[16,128,128]{2,1,0:T(8,128)(2,1)S(1)}, bf16[16,128,128]{2,1,0:T(8,128)(2,1)S(1)}, u32[]{:S(2)}, u32[]{:S(2)}) %collective-permute-start.4) | collective-permute-done | bytes 524320 | tf_op jit(solution)/shard_map/ppermute | solution.py:20
  156.5 2.3 collective-permute-done.5
  158.8 0.2 fusion.10
  159.1 0.2 convert_element_type.37
  159.2 1.3 copy.44
  160.5 0.2 slice.201
  160.7 8.2 %collective-permute-done.2 = bf16[16,128,128]{2,1,0:T(8,128)(2,1)} collective-permute-done((bf16[16,128,128]{2,1,0:T(8,128)(2,1)}, bf16[16,128,128]{2,1,0:T(8,128)(2,1)}, u32[]{:S(2)}, u32[]{:S(2)}) %collective-permute-start.2) | collective-permute-done | bytes 524320 | tf_op jit(solution)/shard_map/ppermute | solution.py:20
  169.0 2.8 pad_maximum_fusion.1.kv_ref
  171.8 4.8 %all-to-all-start.4 = ((bf16[4,1024,128]{1,2,0:T(8,128)(2,1)}), bf16[4,1024,128]{1,2,0:T(8,128)(2,1)}, u32[]{:S(2)}, u32[]{:S(2)}) async-start(bf16[4,1024,128]{1,2,0:T(8,128)(2,1)} %copy.44), calls=%async_computation.4 | async-start | bytes 2097152 | tf_op jit(solution)/shard_map/all_to_all | solution.py:140
  176.5 1.6 copy-done.4
  178.1 49.2 %shard_map.87 = (bf16[32,128,128]{2,1,0:T(8,128)(2,1)S(1)}, f32[64,128,128]{2,1,0:T(8,128)}) custom-call(s32[256]{0:T(256)S(1)} %reshape.197.lists, s32[256]{0:T(256)S(1)} %reshape.198.list_counts, bf16[32,128,256]{2,1,0:T(8,128)(2,1)S(1)} %bitcast.32, bf16[64,128,128]{2,1,0:T(8,128)(2,1)S(1)} %copy-done.4), custom_call_target="tpu_custom_call" | custom-call | flops 107374182400 | bytes 8388608 | tf_op jit(solution)/shard_map/pallas_call | solution.py:198
  227.3 1.3 copy.42
  228.6 5.1 %all-to-all-start.3 = ((bf16[4,1024,128]{1,2,0:T(8,128)(2,1)}), bf16[4,1024,128]{1,2,0:T(8,128)(2,1)S(1)}, u32[]{:S(2)}, u32[]{:S(2)}) async-start(bf16[4,1024,128]{1,2,0:T(8,128)(2,1)} %copy.42), calls=%async_computation.3 | async-start | bytes 2097152 | tf_op jit(solution)/shard_map/all_to_all | solution.py:140
  233.7 2.7 convert.9
  236.5 0.2 collective-permute-start.6
  236.7 0.4 collective-permute-start.7
  237.2 0.2 slice.187
  237.4 10.8 %collective-permute-done.6 = bf16[16,128,128]{2,1,0:T(8,128)(2,1)S(1)} collective-permute-done((bf16[16,128,128]{2,1,0:T(8,128)(2,1)S(1)}, bf16[16,128,128]{2,1,0:T(8,128)(2,1)S(1)}, u32[]{:S(2)}, u32[]{:S(2)}) %collective-permute-start.6) | collective-permute-done | bytes 524320 | tf_op jit(solution)/shard_map/ppermute | solution.py:20
  248.4 2.5 collective-permute-done.7
  250.9 0.2 fusion.9
  251.1 0.2 convert_element_type.40
  251.3 1.3 copy.45
  252.6 5.6 %all-to-all-done.3 = bf16[4,1024,128]{1,2,0:T(8,128)(2,1)S(1)} async-done(((bf16[4,1024,128]{1,2,0:T(8,128)(2,1)}), bf16[4,1024,128]{1,2,0:T(8,128)(2,1)S(1)}, u32[]{:S(2)}, u32[]{:S(2)}) %all-to-all-start.3) | async-done | bytes 1048608 | tf_op jit(solution)/shard_map/all_to_all | solution.py:140
  258.2 3.5 %all-to-all-start.5 = ((bf16[4,1024,128]{1,2,0:T(8,128)(2,1)}), bf16[4,1024,128]{1,2,0:T(8,128)(2,1)S(1)}, u32[]{:S(2)}, u32[]{:S(2)}) async-start(bf16[4,1024,128]{1,2,0:T(8,128)(2,1)} %copy.45), calls=%async_computation.5 | async-start | bytes 2097152 | tf_op jit(solution)/shard_map/all_to_all | solution.py:140
  261.7 2.1 fusion.27
  263.8 0.9 fusion.26
  264.9 1.0 copy-done.11
  265.9 0.4 copy-done.3
  266.2 1.5 fusion.8
  267.7 1.3 reshape.208
  269.0 0.9 copy.46
  269.9 17.0 %all-to-all-done.5 = bf16[4,1024,128]{1,2,0:T(8,128)(2,1)S(1)} async-done(((bf16[4,1024,128]{1,2,0:T(8,128)(2,1)}), bf16[4,1024,128]{1,2,0:T(8,128)(2,1)S(1)}, u32[]{:S(2)}, u32[]{:S(2)}) %all-to-all-start.5) | async-done | bytes 1048608 | tf_op jit(solution)/shard_map/all_to_all | solution.py:140
  286.9 4.5 %all-to-all-start.6 = ((bf16[16,128,128]{2,1,0:T(8,128)(2,1)}), bf16[16,128,128]{2,1,0:T(8,128)(2,1)S(1)}, u32[]{:S(2)}, u32[]{:S(2)}) async-start(bf16[16,128,128]{2,1,0:T(8,128)(2,1)} %bitcast.16), calls=%async_computation.6 | async-start | bytes 1048576 | tf_op jit(solution)/shard_map/all_to_all | solution.py:264
  291.5 2.5 fusion.1
  294.0 1.7 select_convert_fusion
  295.8 2.0 fusion
  297.7 9.4 %all-to-all-done.6 = bf16[16,128,128]{2,1,0:T(8,128)(2,1)S(1)} async-done(((bf16[16,128,128]{2,1,0:T(8,128)(2,1)}), bf16[16,128,128]{2,1,0:T(8,128)(2,1)S(1)}, u32[]{:S(2)}, u32[]{:S(2)}) %all-to-all-start.6) | async-done | bytes 524320 | tf_op jit(solution)/shard_map/all_to_all | solution.py:264
  307.1 0.7 convert_reduce_fusion
  (52 shorter events, 1.2 us)
Async XLA Ops:
  0.6 2.4 copy-start.17
  3.5 3.5 %copy-start.15 = (pred[1024]{0:T(1024)(128)(4,1)}, pred[1024]{0:T(1024)(128)(4,1)S(1)}, u32[]{:S(2)}) copy-start(pred[1024]{0:T(1024)(128)(4,1)S(1)} %fusion.13) | copy-start | bytes 3076
  4.9 3.5 %copy-start.5 = (bf16[1024,512]{1,0:T(8,128)(2,1)S(1)}, bf16[1024,512]{1,0:T(8,128)(2,1)}, u32[]{:S(2)}) copy-start(bf16[1024,512]{1,0:T(8,128)(2,1)} %x_ref.1) | copy-start | bytes 3145732
  4.9 3.5 %copy-start.6 = (bf16[512,512]{1,0:T(8,128)(2,1)S(1)}, bf16[512,512]{1,0:T(8,128)(2,1)}, u32[]{:S(2)}) copy-start(bf16[512,512]{1,0:T(8,128)(2,1)} %wo_ref.1) | copy-start | bytes 1572868
  8.4 5.3 %copy-start.2 = (bf16[1024,512]{1,0:T(8,128)(2,1)}, bf16[1024,512]{1,0:T(8,128)(2,1)S(1)}, u32[]{:S(2)}) copy-start(bf16[1024,512]{1,0:T(8,128)(2,1)S(1)} %broadcast_select_fusion.g_ref) | copy-start | bytes 3145732
  68.2 4.4 %copy-start = (bf16[4,1024,256]{2,1,0:T(8,128)(2,1)}, bf16[4,1024,256]{2,1,0:T(8,128)(2,1)S(1)}, u32[]{:S(2)}) copy-start(bf16[4,1024,256]{2,1,0:T(8,128)(2,1)S(1)} %all_to_all.35) | copy-start | bytes 6291460
  68.2 3.1 %copy-start.14 = (s32[32,8]{0,1:T(8,128)S(1)}, s32[32,8]{0,1:T(8,128)}, u32[]{:S(2)}) copy-start(s32[32,8]{0,1:T(8,128)} %param.17) | copy-start | bytes 3076
  69.5 12.7 %collective-permute-start = (bf16[16,128,128]{2,1,0:T(8,128)(2,1)}, bf16[16,128,128]{2,1,0:T(8,128)(2,1)}, u32[]{:S(2)}, u32[]{:S(2)}) collective-permute-start(bf16[16,128,128]{2,1,0:T(8,128)(2,1)} %get-tuple-element.69), channel_id=1, source_target_pairs={{0,4},{4,8},{8,12},{12,0},{1,5},{5,9},{9,13},{13,1},{2,6},{6,10},{... | collective-permute-start | bytes 1572872 | tf_op jit(solution)/shard_map/ppermute | solution.py:20
  69.5 13.5 %collective-permute-start.1 = (bf16[16,128,128]{2,1,0:T(8,128)(2,1)}, bf16[16,128,128]{2,1,0:T(8,128)(2,1)}, u32[]{:S(2)}, u32[]{:S(2)}) collective-permute-start(bf16[16,128,128]{2,1,0:T(8,128)(2,1)} %get-tuple-element.70), channel_id=1, source_target_pairs={{0,12},{4,0},{8,4},{12,8},{1,13},{5,1},{9,5},{13,9},{2,14},{6,2},{... | collective-permute-start | bytes 1572872 | tf_op jit(solution)/shard_map/ppermute | solution.py:20
  72.5 62.5 %all-to-all-start.2 = ((bf16[4,1024,256]{2,1,0:T(8,128)(2,1)}), bf16[4,1024,256]{2,1,0:T(8,128)(2,1)S(1)}, u32[]{:S(2)}, u32[]{:S(2)}) async-start(bf16[4,1024,256]{2,1,0:T(8,128)(2,1)} %get-tuple-element.61), calls=%async_computation.2 | async-start | bytes 4194304 | tf_op jit(solution)/shard_map/all_to_all | solution.py:140
  76.2 8.4 %copy-start.1 = (bf16[4,1024,256]{2,1,0:T(8,128)(2,1)S(1)}, bf16[4,1024,256]{2,1,0:T(8,128)(2,1)}, u32[]{:S(2)}) copy-start(bf16[4,1024,256]{2,1,0:T(8,128)(2,1)} %copy-done) | copy-start | bytes 6291460
  135.0 36.7 %all-to-all-start.1 = ((bf16[4,1024,128]{1,2,0:T(8,128)(2,1)}), bf16[4,1024,128]{1,2,0:T(8,128)(2,1)}, u32[]{:S(2)}, u32[]{:S(2)}) async-start(bf16[4,1024,128]{1,2,0:T(8,128)(2,1)} %copy.41), calls=%async_computation.1 | async-start | bytes 2097152 | tf_op jit(solution)/shard_map/all_to_all | solution.py:140
  139.3 5.0 %copy-start.8 = (f32[64,128,128]{2,1,0:T(8,128)S(1)}, f32[64,128,128]{2,1,0:T(8,128)}, u32[]{:S(2)}) copy-start(f32[64,128,128]{2,1,0:T(8,128)} %get-tuple-element.63) | copy-start | bytes 12582916
  142.2 14.2 %collective-permute-start.4 = (bf16[16,128,128]{2,1,0:T(8,128)(2,1)S(1)}, bf16[16,128,128]{2,1,0:T(8,128)(2,1)S(1)}, u32[]{:S(2)}, u32[]{:S(2)}) collective-permute-start(bf16[16,128,128]{2,1,0:T(8,128)(2,1)S(1)} %get-tuple-element.68), channel_id=1, source_target_pairs={{0,12},{4,0},{8,4},{12,8},{1,13},{5,1},{9,5},{13,9},{2,14},{6,2},{... | collective-permute-start | bytes 1572872 | tf_op jit(solution)/shard_map/ppermute | solution.py:20
  144.5 14.3 %collective-permute-start.5 = (bf16[16,128,128]{2,1,0:T(8,128)(2,1)S(1)}, bf16[16,128,128]{2,1,0:T(8,128)(2,1)S(1)}, u32[]{:S(2)}, u32[]{:S(2)}) collective-permute-start(bf16[16,128,128]{2,1,0:T(8,128)(2,1)S(1)} %get-tuple-element.67), channel_id=1, source_target_pairs={{0,4},{4,8},{8,12},{12,0},{1,5},{5,9},{9,13},{13,1},{2,6},{6,10},{... | collective-permute-start | bytes 1572872 | tf_op jit(solution)/shard_map/ppermute | solution.py:20
  145.8 23.2 %collective-permute-start.2 = (bf16[16,128,128]{2,1,0:T(8,128)(2,1)}, bf16[16,128,128]{2,1,0:T(8,128)(2,1)}, u32[]{:S(2)}, u32[]{:S(2)}) collective-permute-start(bf16[16,128,128]{2,1,0:T(8,128)(2,1)} %get-tuple-element.71), channel_id=1, source_target_pairs={{0,4},{4,8},{8,12},{12,0},{1,5},{5,9},{9,13},{13,1},{2,6},{6,10},{... | collective-permute-start | bytes 1572872 | tf_op jit(solution)/shard_map/ppermute | solution.py:20
  146.4 22.6 %collective-permute-start.3 = (bf16[16,128,128]{2,1,0:T(8,128)(2,1)}, bf16[16,128,128]{2,1,0:T(8,128)(2,1)}, u32[]{:S(2)}, u32[]{:S(2)}) collective-permute-start(bf16[16,128,128]{2,1,0:T(8,128)(2,1)} %get-tuple-element.72), channel_id=1, source_target_pairs={{0,12},{4,0},{8,4},{12,8},{1,13},{5,1},{9,5},{13,9},{2,14},{6,2},{... | collective-permute-start | bytes 1572872 | tf_op jit(solution)/shard_map/ppermute | solution.py:20
  171.8 56.9 %all-to-all-start.4 = ((bf16[4,1024,128]{1,2,0:T(8,128)(2,1)}), bf16[4,1024,128]{1,2,0:T(8,128)(2,1)}, u32[]{:S(2)}, u32[]{:S(2)}) async-start(bf16[4,1024,128]{1,2,0:T(8,128)(2,1)} %copy.44), calls=%async_computation.4 | async-start | bytes 2097152 | tf_op jit(solution)/shard_map/all_to_all | solution.py:140
  176.5 1.6 copy-start.4
  228.6 29.5 %all-to-all-start.3 = ((bf16[4,1024,128]{1,2,0:T(8,128)(2,1)}), bf16[4,1024,128]{1,2,0:T(8,128)(2,1)S(1)}, u32[]{:S(2)}, u32[]{:S(2)}) async-start(bf16[4,1024,128]{1,2,0:T(8,128)(2,1)} %copy.42), calls=%async_computation.3 | async-start | bytes 2097152 | tf_op jit(solution)/shard_map/all_to_all | solution.py:140
  233.7 3.4 %copy-start.9 = (f32[64,128,128]{2,1,0:T(8,128)S(1)}, f32[64,128,128]{2,1,0:T(8,128)}, u32[]{:S(2)}) copy-start(f32[64,128,128]{2,1,0:T(8,128)} %get-tuple-element.64) | copy-start | bytes 12582916
  236.5 11.7 %collective-permute-start.6 = (bf16[16,128,128]{2,1,0:T(8,128)(2,1)S(1)}, bf16[16,128,128]{2,1,0:T(8,128)(2,1)S(1)}, u32[]{:S(2)}, u32[]{:S(2)}) collective-permute-start(bf16[16,128,128]{2,1,0:T(8,128)(2,1)S(1)} %get-tuple-element.66), channel_id=1, source_target_pairs={{0,12},{4,0},{8,4},{12,8},{1,13},{5,1},{9,5},{13,9},{2,14},{6,2},{... | collective-permute-start | bytes 1572872 | tf_op jit(solution)/shard_map/ppermute | solution.py:20
  236.7 14.1 %collective-permute-start.7 = (bf16[16,128,128]{2,1,0:T(8,128)(2,1)S(1)}, bf16[16,128,128]{2,1,0:T(8,128)(2,1)S(1)}, u32[]{:S(2)}, u32[]{:S(2)}) collective-permute-start(bf16[16,128,128]{2,1,0:T(8,128)(2,1)S(1)} %get-tuple-element.65), channel_id=1, source_target_pairs={{0,4},{4,8},{8,12},{12,0},{1,5},{5,9},{9,13},{13,1},{2,6},{6,10},{... | collective-permute-start | bytes 1572872 | tf_op jit(solution)/shard_map/ppermute | solution.py:20
  258.2 28.7 %all-to-all-start.5 = ((bf16[4,1024,128]{1,2,0:T(8,128)(2,1)}), bf16[4,1024,128]{1,2,0:T(8,128)(2,1)S(1)}, u32[]{:S(2)}, u32[]{:S(2)}) async-start(bf16[4,1024,128]{1,2,0:T(8,128)(2,1)} %copy.45), calls=%async_computation.5 | async-start | bytes 2097152 | tf_op jit(solution)/shard_map/all_to_all | solution.py:140
  264.7 1.5 copy-start.3
  264.9 1.0 copy-start.11
  267.7 23.7 %copy-start.10 = (bf16[4,512,2,3,2,32]{1,5,4,3,2,0:T(8,128)(2,1)S(1)}, bf16[4,512,2,3,2,32]{1,5,4,3,2,0:T(8,128)(2,1)}, u32[]{:S(2)}) copy-start(bf16[4,512,2,3,2,32]{1,5,4,3,2,0:T(8,128)(2,1)} %copy.39) | copy-start | bytes 4718596
  286.9 20.2 %all-to-all-start.6 = ((bf16[16,128,128]{2,1,0:T(8,128)(2,1)}), bf16[16,128,128]{2,1,0:T(8,128)(2,1)S(1)}, u32[]{:S(2)}, u32[]{:S(2)}) async-start(bf16[16,128,128]{2,1,0:T(8,128)(2,1)} %bitcast.16), calls=%async_computation.6 | async-start | bytes 1048576 | tf_op jit(solution)/shard_map/all_to_all | solution.py:264
  291.4 2.6 copy-start.7
  291.5 2.6 copy-start.12
  291.5 2.5 copy-start.16
  294.0 1.7 copy-start.13

commit v3 on v2

--- a/solution.py
+++ b/solution.py
@@ -11,7 +11,7 @@
 BLOCK = 128
 NEIGH = 8
 REACH = 16
-TOGETHER = 2
+TOGETHER = 4
 VMEM_BYTES = 48 * 1024 * 1024
 
 
@@ -41,13 +41,14 @@
 
 
 def attention_kernel(
-    heads, lists, list_counts, own_ref, kv_ref, out_ref, dkv_ref,
-    turned_ref, l_ref, lt_ref, s_ref, p_ref, g_ref, sum_ref,
+    heads, lists, list_counts, own_ref, kv_ref, out_ref, low_ref, dkv_ref, high_ref,
+    acc_ref, turned_ref, l_ref, lt_ref, s_ref, p_ref, g_ref, sum_ref,
 ):
     step = pl.program_id(0)
     together = own_ref.shape[0]
     ext_blocks = kv_ref.shape[0]
     width = out_ref.shape[2] // 2
+    own_blocks = dkv_ref.shape[0]
     head_dim = width // heads
     lanes = heads * BLOCK
     scale = 1.0 / math.sqrt(head_dim)
@@ -57,7 +58,7 @@
 
     @pl.when(step == 0)
     def _():
-        dkv_ref[...] = jnp.zeros_like(dkv_ref)
+        acc_ref[...] = jnp.zeros_like(acc_ref)
 
         @pl.loop(0, ext_blocks)
         def _(block):
@@ -133,7 +134,13 @@
         out_ref[u] = jnp.concatenate(rows, axis=0).T.astype(bf16)
     for u in each:
         for n in range(NEIGH):
-            dkv_ref[ids[u][n]] += sum_ref[u, spans[n]]
+            acc_ref[ids[u][n]] += sum_ref[u, spans[n]]
+
+    @pl.when(step == pl.num_programs(0) - 1)
+    def _():
+        low_ref[...] = acc_ref[:REACH].astype(bf16)
+        dkv_ref[...] = acc_ref[REACH : REACH + own_blocks]
+        high_ref[...] = acc_ref[REACH + own_blocks :].astype(bf16)
 
 
 def exchange(blocks):
@@ -206,9 +213,12 @@
                 ],
                 out_specs=[
                     pl.BlockSpec((TOGETHER, BLOCK, 2 * width), lambda b, *_: (b, 0, 0)),
-                    pl.BlockSpec((ext_blocks, BLOCK, 2 * width), lambda b, *_: (0, 0, 0)),
+                    pl.BlockSpec((REACH, BLOCK, 2 * width), lambda b, *_: (0, 0, 0)),
+                    pl.BlockSpec((slab_blocks, BLOCK, 2 * width), lambda b, *_: (0, 0, 0)),
+                    pl.BlockSpec((REACH, BLOCK, 2 * width), lambda b, *_: (0, 0, 0)),
                 ],
                 scratch_shapes=[
+                    pltpu.VMEM((ext_blocks, BLOCK, 2 * width), jnp.float32),
                     pltpu.VMEM((ext_blocks, 2 * width, BLOCK), bf16),
                     pltpu.VMEM((TOGETHER, list_rows, 2 * width), bf16),
                     pltpu.VMEM((TOGETHER, 2 * width, list_rows), bf16),
@@ -220,7 +230,9 @@
             ),
             out_shape=[
                 jax.ShapeDtypeStruct((slab_blocks, BLOCK, 2 * width), bf16),
-                jax.ShapeDtypeStruct((ext_blocks, BLOCK, 2 * width), jnp.float32),
+                jax.ShapeDtypeStruct((REACH, BLOCK, 2 * width), bf16),
+                jax.ShapeDtypeStruct((slab_blocks, BLOCK, 2 * width), jnp.float32),
+                jax.ShapeDtypeStruct((REACH, BLOCK, 2 * width), bf16),
             ],
             compiler_params=pltpu.CompilerParams(vmem_limit_bytes=VMEM_BYTES),
             cost_estimate=pl.CostEstimate(
@@ -242,11 +254,10 @@
         results.append(attend(own, before, after))
 
     att_dq, grad_kv_rows = [], []
-    for rows, grad_kv in results:
-        from_next = from_behind(grad_kv[:REACH].astype(bf16), "slab", -1)
-        from_prev = from_behind(grad_kv[REACH + slab_blocks :].astype(bf16), "slab", 1)
+    for rows, low, own_grad, high in results:
+        from_next = from_behind(low, "slab", -1)
+        from_prev = from_behind(high, "slab", 1)
         att_dq.append(exchange(rows.reshape(n_head, row_count, 2 * width)))
-        own_grad = grad_kv[REACH : REACH + slab_blocks]
         own_grad = own_grad.at[slab_blocks - REACH :].add(from_next.astype(jnp.float32))
         own_grad = own_grad.at[:REACH].add(from_prev.astype(jnp.float32))
         own_grad = own_grad.astype(bf16).reshape(n_head, row_count, 2 * width)

time: 309 us -> 303 us (0.981)
  Pallas kernels: 104 us -> 97 us
  local copies, waits for them, and re-layouts: 23.1 us -> 27.6 us
  other arithmetic: 14.1 us -> 10.3 us
    pallas_call x2, Pallas kernels: 98.4 us -> 91.7 us  [attend(): pl.pallas_call(functools.partial(attention_kernel, heads), grid_spec=pltp...]
    another operation x2 -> x0, other arithmetic: 5.41 us -> none
  transfers between devices with their start and end apart: 14 -> 14, of which waited for: 10 -> 10; matrix products, arithmetic and copies ran while one was open for 10% -> 10% of each run, Pallas kernels for 32% -> 30%
where the time goes in v3:
time: 303 us; the launch traced here: 302 us
  Pallas kernels  97 us (32%)
  waiting for transfers between devices  70.7 us (23%)
  blocking collectives  54.5 us (18%)
  starting transfers between devices  33.2 us (11%)
  local copies, waits for them, and re-layouts  27.6 us (9%)
  other arithmetic  10.3 us (3%)
  matrix products  7.71 us (3%)
    pallas_call x2, Pallas kernels, attend(): pl.pallas_call(functools.partial(attention_kernel, heads), grid_spec=pltp...  91.7 us
    all_to_all x1, blocking collectives, exchange(): lax.all_to_all(blocks, 'head', split_axis=0, concat_axis=0, tiled=True)  54.5 us
    ppermute x8, waiting for transfers between devices, from_behind(): lax.ppermute(shard, axis, [(i, (i + by) % count) for i in range(count)])  36.9 us
    all_to_all x5, waiting for transfers between devices, exchange(): lax.all_to_all(blocks, 'head', split_axis=0, concat_axis=0, tiled=True)  24.4 us
    all_to_all x5, starting transfers between devices, exchange(): lax.all_to_all(blocks, 'head', split_axis=0, concat_axis=0, tiled=True)  22.3 us
    all_to_all x1, waiting for transfers between devices, on_device(): lax.all_to_all(term, ('slab', 'head'), split_axis=0, concat_axis=0, tiled...  9.39 us
    ppermute x8, starting transfers between devices, from_behind(): lax.ppermute(shard, axis, [(i, (i + by) % count) for i in range(count)])  6.26 us
  transfers between devices with their start and end apart: 14, of which 10 were waited for; matrix products, arithmetic and copies ran while one was open for 10% of the time, Pallas kernels for 30%

profile of v3, /device:TPU:0, one launch (start us, length us, event | category | flops | bytes accessed | tf_op | source)
XLA Modules:
  0.0 302.0 jit_solution(7726984115267304529)
XLA Ops:
  0.6 1.3 slice.164
  2.0 1.1 slice.165
  3.1 0.4 select_reduce_fusion
  3.6 1.3 copy.39
  4.9 2.0 copy.40.w_ref
  6.9 1.4 broadcast_select_fusion.g_ref
  8.4 5.3 %shard_map.85 = (bf16[4,1024,256]{2,1,0:T(8,128)(2,1)}, bf16[4,1024,256]{2,1,0:T(8,128)(2,1)}) custom-call(bf16[1024,512]{1,0:T(8,128)(2,1)S(1)} %copy-done.2, bf16[1024,512]{1,0:T(8,128)(2,1)S(1)} %broadcast_select_fusion.g_ref, bf16[4,512,384]{2,1,0:T(8,128)(2,1)S(1)} %copy.40.w_ref, bf16[512,512]{1,0:T(8,128)(2,1)S(1)} %copy-done.3), custom_call_target="tpu_custom_call" | custom-call | tf_op jit(solution)/shard_map/pallas_call | solution.py:185
  13.7 54.5 %all_to_all.35 = bf16[4,1024,256]{2,1,0:T(8,128)(2,1)S(1)} all-to-all(bf16[4,1024,256]{2,1,0:T(8,128)(2,1)} %get-tuple-element.62), channel_id=1, replica_groups=mesh['rep'=2,'slab'=4,'head'=4] {'head'}, dimensions={0} | all-to-all | bytes 4194304 | tf_op jit(solution)/shard_map/all_to_all | solution.py:147
  68.2 1.4 fusion.22
  69.6 1.7 collective-permute-start.1
  71.6 0.7 select_reduce_fusion.1
  72.4 0.2 slice.167
  72.6 4.5 %all-to-all-start.2 = ((bf16[4,1024,256]{2,1,0:T(8,128)(2,1)}), bf16[4,1024,256]{2,1,0:T(8,128)(2,1)}, u32[]{:S(2)}, u32[]{:S(2)}) async-start(bf16[4,1024,256]{2,1,0:T(8,128)(2,1)} %get-tuple-element.65), calls=%async_computation.2 | async-start | bytes 4194304 | tf_op jit(solution)/shard_map/all_to_all | solution.py:147
  77.1 5.2 %collective-permute-done = bf16[16,128,128]{2,1,0:T(8,128)(2,1)} collective-permute-done((bf16[16,128,128]{2,1,0:T(8,128)(2,1)}, bf16[16,128,128]{2,1,0:T(8,128)(2,1)}, u32[]{:S(2)}, u32[]{:S(2)}) %collective-permute-start) | collective-permute-done | bytes 524320 | tf_op jit(solution)/shard_map/ppermute | solution.py:20
  82.3 0.9 collective-permute-done.1
  83.2 2.8 pad_maximum_fusion.kv_ref
  86.0 45.8 %shard_map.86 = (bf16[32,128,128]{2,1,0:T(8,128)(2,1)S(1)}, bf16[16,128,128]{2,1,0:T(8,128)(2,1)S(1)}, f32[32,128,128]{2,1,0:T(8,128)S(1)}, bf16[16,128,128]{2,1,0:T(8,128)(2,1)S(1)}) custom-call(s32[256]{0:T(256)S(1)} %reshape.197.lists, s32[256]{0:T(256)S(1)} %reshape.198.list_counts, bf16[32,128,256]{2,1,0:T(8,128)(2,1)} %bitcast.34, ...), custom_call_target="tpu_custom_call" | custom-call | flops 107374182400 | bytes 8388608 | tf_op jit(solution)/shard_map/pallas_call | solution.py:205
  131.9 0.8 copy-done.5
  132.7 0.8 copy-done.7
  133.4 1.3 copy.41
  134.8 4.4 %all-to-all-start.1 = ((bf16[4,1024,128]{1,2,0:T(8,128)(2,1)}), bf16[4,1024,128]{1,2,0:T(8,128)(2,1)}, u32[]{:S(2)}, u32[]{:S(2)}) async-start(bf16[4,1024,128]{1,2,0:T(8,128)(2,1)} %copy.41), calls=%async_computation.1 | async-start | bytes 2097152 | tf_op jit(solution)/shard_map/all_to_all | solution.py:147
  139.2 2.3 collective-permute-start.4
  141.4 2.3 fusion.23
  143.7 0.6 collective-permute-start.2
  144.4 1.1 collective-permute-start.3
  145.5 8.3 %collective-permute-done.4 = bf16[16,128,128]{2,1,0:T(8,128)(2,1)S(1)} collective-permute-done((bf16[16,128,128]{2,1,0:T(8,128)(2,1)S(1)}, bf16[16,128,128]{2,1,0:T(8,128)(2,1)S(1)}, u32[]{:S(2)}, u32[]{:S(2)}) %collective-permute-start.4) | collective-permute-done | bytes 524320 | tf_op jit(solution)/shard_map/ppermute | solution.py:20
  153.7 0.2 add_dynamic-update-slice_fusion.1
  154.0 1.7 collective-permute-done.5
  155.6 0.2 fusion.10
  155.9 0.2 convert_element_type.33
  156.0 1.3 copy.44
  157.4 1.3 slice.171
  158.7 7.4 %collective-permute-done.2 = bf16[16,128,128]{2,1,0:T(8,128)(2,1)} collective-permute-done((bf16[16,128,128]{2,1,0:T(8,128)(2,1)}, bf16[16,128,128]{2,1,0:T(8,128)(2,1)}, u32[]{:S(2)}, u32[]{:S(2)}) %collective-permute-start.2) | collective-permute-done | bytes 524320 | tf_op jit(solution)/shard_map/ppermute | solution.py:20
  166.1 2.8 pad_maximum_fusion.1.kv_ref
  168.9 4.7 %all-to-all-start.4 = ((bf16[4,1024,128]{1,2,0:T(8,128)(2,1)}), bf16[4,1024,128]{1,2,0:T(8,128)(2,1)}, u32[]{:S(2)}, u32[]{:S(2)}) async-start(bf16[4,1024,128]{1,2,0:T(8,128)(2,1)} %copy.44), calls=%async_computation.4 | async-start | bytes 2097152 | tf_op jit(solution)/shard_map/all_to_all | solution.py:147
  173.6 45.8 %shard_map.87 = (bf16[32,128,128]{2,1,0:T(8,128)(2,1)S(1)}, bf16[16,128,128]{2,1,0:T(8,128)(2,1)S(1)}, f32[32,128,128]{2,1,0:T(8,128)S(1)}, bf16[16,128,128]{2,1,0:T(8,128)(2,1)S(1)}) custom-call(s32[256]{0:T(256)S(1)} %reshape.197.lists, s32[256]{0:T(256)S(1)} %reshape.198.list_counts, bf16[32,128,256]{2,1,0:T(8,128)(2,1)} %bitcast.6.own_ref, ...), custom_call_target="tpu_custom_call" | custom-call | flops 107374182400 | bytes 8388608 | tf_op jit(solution)/shard_map/pallas_call | solution.py:205
  219.4 0.8 copy-done.9
  220.3 0.8 copy-done.11
  221.1 1.3 copy.42
  222.4 5.2 %all-to-all-start.3 = ((bf16[4,1024,128]{1,2,0:T(8,128)(2,1)}), bf16[4,1024,128]{1,2,0:T(8,128)(2,1)}, u32[]{:S(2)}, u32[]{:S(2)}) async-start(bf16[4,1024,128]{1,2,0:T(8,128)(2,1)} %copy.42), calls=%async_computation.3 | async-start | bytes 2097152 | tf_op jit(solution)/shard_map/all_to_all | solution.py:147
  227.6 0.3 collective-permute-start.6
  227.9 0.2 collective-permute-start.7
  228.2 11.5 %collective-permute-done.6 = bf16[16,128,128]{2,1,0:T(8,128)(2,1)S(1)} collective-permute-done((bf16[16,128,128]{2,1,0:T(8,128)(2,1)S(1)}, bf16[16,128,128]{2,1,0:T(8,128)(2,1)S(1)}, u32[]{:S(2)}, u32[]{:S(2)}) %collective-permute-start.6) | collective-permute-done | bytes 524320 | tf_op jit(solution)/shard_map/ppermute | solution.py:20
  239.7 0.2 add_dynamic-update-slice_fusion
  239.9 1.9 collective-permute-done.7
  241.8 0.2 fusion.9
  242.1 0.2 convert_element_type.36
  242.2 1.3 copy.45
  243.6 8.7 %all-to-all-done.3 = bf16[4,1024,128]{1,2,0:T(8,128)(2,1)} async-done(((bf16[4,1024,128]{1,2,0:T(8,128)(2,1)}), bf16[4,1024,128]{1,2,0:T(8,128)(2,1)}, u32[]{:S(2)}, u32[]{:S(2)}) %all-to-all-start.3) | async-done | bytes 1048608 | tf_op jit(solution)/shard_map/all_to_all | solution.py:147
  252.3 3.5 %all-to-all-start.5 = ((bf16[4,1024,128]{1,2,0:T(8,128)(2,1)}), bf16[4,1024,128]{1,2,0:T(8,128)(2,1)S(1)}, u32[]{:S(2)}, u32[]{:S(2)}) async-start(bf16[4,1024,128]{1,2,0:T(8,128)(2,1)} %copy.45), calls=%async_computation.5 | async-start | bytes 2097152 | tf_op jit(solution)/shard_map/all_to_all | solution.py:147
  255.8 2.1 fusion.25
  258.0 2.1 fusion.24
  260.3 1.0 copy-done.15
  261.2 0.4 copy-done.1
  261.6 1.5 fusion.8
  263.1 1.3 reshape.208
  264.4 0.9 copy.46
  265.3 15.7 %all-to-all-done.5 = bf16[4,1024,128]{1,2,0:T(8,128)(2,1)S(1)} async-done(((bf16[4,1024,128]{1,2,0:T(8,128)(2,1)}), bf16[4,1024,128]{1,2,0:T(8,128)(2,1)S(1)}, u32[]{:S(2)}, u32[]{:S(2)}) %all-to-all-start.5) | async-done | bytes 1048608 | tf_op jit(solution)/shard_map/all_to_all | solution.py:147
  281.0 4.6 %all-to-all-start.6 = ((bf16[16,128,128]{2,1,0:T(8,128)(2,1)}), bf16[16,128,128]{2,1,0:T(8,128)(2,1)S(1)}, u32[]{:S(2)}, u32[]{:S(2)}) async-start(bf16[16,128,128]{2,1,0:T(8,128)(2,1)} %bitcast.16), calls=%async_computation.6 | async-start | bytes 1048576 | tf_op jit(solution)/shard_map/all_to_all | solution.py:275
  285.7 2.5 fusion.1
  288.2 1.7 select_convert_fusion
  289.9 2.0 fusion
  291.9 9.4 %all-to-all-done.6 = bf16[16,128,128]{2,1,0:T(8,128)(2,1)S(1)} async-done(((bf16[16,128,128]{2,1,0:T(8,128)(2,1)}), bf16[16,128,128]{2,1,0:T(8,128)(2,1)S(1)}, u32[]{:S(2)}, u32[]{:S(2)}) %all-to-all-start.6) | async-done | bytes 524320 | tf_op jit(solution)/shard_map/all_to_all | solution.py:275
  301.3 0.7 convert_reduce_fusion
  (54 shorter events, 0.8 us)
Async XLA Ops:
  0.6 2.4 copy-start.21
  3.5 3.5 %copy-start.19 = (pred[1024]{0:T(1024)(128)(4,1)}, pred[1024]{0:T(1024)(128)(4,1)S(1)}, u32[]{:S(2)}) copy-start(pred[1024]{0:T(1024)(128)(4,1)S(1)} %fusion.13) | copy-start | bytes 3076
  4.9 3.5 %copy-start.2 = (bf16[1024,512]{1,0:T(8,128)(2,1)S(1)}, bf16[1024,512]{1,0:T(8,128)(2,1)}, u32[]{:S(2)}) copy-start(bf16[1024,512]{1,0:T(8,128)(2,1)} %x_ref.1) | copy-start | bytes 3145732
  4.9 3.5 %copy-start.3 = (bf16[512,512]{1,0:T(8,128)(2,1)S(1)}, bf16[512,512]{1,0:T(8,128)(2,1)}, u32[]{:S(2)}) copy-start(bf16[512,512]{1,0:T(8,128)(2,1)} %wo_ref.1) | copy-start | bytes 1572868
  8.4 5.3 %copy-start = (bf16[1024,512]{1,0:T(8,128)(2,1)}, bf16[1024,512]{1,0:T(8,128)(2,1)S(1)}, u32[]{:S(2)}) copy-start(bf16[1024,512]{1,0:T(8,128)(2,1)S(1)} %broadcast_select_fusion.g_ref) | copy-start | bytes 3145732
  68.2 4.4 %copy-start.13 = (bf16[4,1024,256]{2,1,0:T(8,128)(2,1)}, bf16[4,1024,256]{2,1,0:T(8,128)(2,1)S(1)}, u32[]{:S(2)}) copy-start(bf16[4,1024,256]{2,1,0:T(8,128)(2,1)S(1)} %all_to_all.35) | copy-start | bytes 6291460
  68.2 3.2 %copy-start.18 = (s32[32,8]{0,1:T(8,128)S(1)}, s32[32,8]{0,1:T(8,128)}, u32[]{:S(2)}) copy-start(s32[32,8]{0,1:T(8,128)} %param.17) | copy-start | bytes 3076
  69.6 12.7 %collective-permute-start = (bf16[16,128,128]{2,1,0:T(8,128)(2,1)}, bf16[16,128,128]{2,1,0:T(8,128)(2,1)}, u32[]{:S(2)}, u32[]{:S(2)}) collective-permute-start(bf16[16,128,128]{2,1,0:T(8,128)(2,1)} %get-tuple-element.73), channel_id=1, source_target_pairs={{0,4},{4,8},{8,12},{12,0},{1,5},{5,9},{9,13},{13,1},{2,6},{6,10},{... | collective-permute-start | bytes 1572872 | tf_op jit(solution)/shard_map/ppermute | solution.py:20
  69.6 13.5 %collective-permute-start.1 = (bf16[16,128,128]{2,1,0:T(8,128)(2,1)}, bf16[16,128,128]{2,1,0:T(8,128)(2,1)}, u32[]{:S(2)}, u32[]{:S(2)}) collective-permute-start(bf16[16,128,128]{2,1,0:T(8,128)(2,1)} %get-tuple-element.74), channel_id=1, source_target_pairs={{0,12},{4,0},{8,4},{12,8},{1,13},{5,1},{9,5},{13,9},{2,14},{6,2},{... | collective-permute-start | bytes 1572872 | tf_op jit(solution)/shard_map/ppermute | solution.py:20
  72.6 62.1 %all-to-all-start.2 = ((bf16[4,1024,256]{2,1,0:T(8,128)(2,1)}), bf16[4,1024,256]{2,1,0:T(8,128)(2,1)}, u32[]{:S(2)}, u32[]{:S(2)}) async-start(bf16[4,1024,256]{2,1,0:T(8,128)(2,1)} %get-tuple-element.65), calls=%async_computation.2 | async-start | bytes 4194304 | tf_op jit(solution)/shard_map/all_to_all | solution.py:147
  131.9 0.8 copy-start.5
  132.7 0.8 copy-start.7
  134.7 4.4 %copy-start.8 = (bf16[16,128,128]{2,1,0:T(8,128)(2,1)S(1)}, bf16[16,128,128]{2,1,0:T(8,128)(2,1)}, u32[]{:S(2)}) copy-start(bf16[16,128,128]{2,1,0:T(8,128)(2,1)} %copy-done.7) | copy-start | bytes 1572868
  134.7 6.7 %copy-start.6 = (bf16[16,128,128]{2,1,0:T(8,128)(2,1)S(1)}, bf16[16,128,128]{2,1,0:T(8,128)(2,1)}, u32[]{:S(2)}) copy-start(bf16[16,128,128]{2,1,0:T(8,128)(2,1)} %copy-done.5) | copy-start | bytes 1572868
  134.8 34.1 %all-to-all-start.1 = ((bf16[4,1024,128]{1,2,0:T(8,128)(2,1)}), bf16[4,1024,128]{1,2,0:T(8,128)(2,1)}, u32[]{:S(2)}, u32[]{:S(2)}) async-start(bf16[4,1024,128]{1,2,0:T(8,128)(2,1)} %copy.41), calls=%async_computation.1 | async-start | bytes 2097152 | tf_op jit(solution)/shard_map/all_to_all | solution.py:147
  139.2 14.6 %collective-permute-start.4 = (bf16[16,128,128]{2,1,0:T(8,128)(2,1)S(1)}, bf16[16,128,128]{2,1,0:T(8,128)(2,1)S(1)}, u32[]{:S(2)}, u32[]{:S(2)}) collective-permute-start(bf16[16,128,128]{2,1,0:T(8,128)(2,1)S(1)} %copy-done.8), channel_id=1, source_target_pairs={{0,12},{4,0},{8,4},{12,8},{1,13},{5,1},{9,5},{13,9},{2,14},{6,2},{... | collective-permute-start | bytes 1572872 | tf_op jit(solution)/shard_map/ppermute | solution.py:20
  141.4 14.2 %collective-permute-start.5 = (bf16[16,128,128]{2,1,0:T(8,128)(2,1)S(1)}, bf16[16,128,128]{2,1,0:T(8,128)(2,1)S(1)}, u32[]{:S(2)}, u32[]{:S(2)}) collective-permute-start(bf16[16,128,128]{2,1,0:T(8,128)(2,1)S(1)} %copy-done.6), channel_id=1, source_target_pairs={{0,4},{4,8},{8,12},{12,0},{1,5},{5,9},{9,13},{13,1},{2,6},{6,10},{... | collective-permute-start | bytes 1572872 | tf_op jit(solution)/shard_map/ppermute | solution.py:20
  143.7 22.4 %collective-permute-start.2 = (bf16[16,128,128]{2,1,0:T(8,128)(2,1)}, bf16[16,128,128]{2,1,0:T(8,128)(2,1)}, u32[]{:S(2)}, u32[]{:S(2)}) collective-permute-start(bf16[16,128,128]{2,1,0:T(8,128)(2,1)} %get-tuple-element.75), channel_id=1, source_target_pairs={{0,4},{4,8},{8,12},{12,0},{1,5},{5,9},{9,13},{13,1},{2,6},{6,10},{... | collective-permute-start | bytes 1572872 | tf_op jit(solution)/shard_map/ppermute | solution.py:20
  144.4 21.7 %collective-permute-start.3 = (bf16[16,128,128]{2,1,0:T(8,128)(2,1)}, bf16[16,128,128]{2,1,0:T(8,128)(2,1)}, u32[]{:S(2)}, u32[]{:S(2)}) collective-permute-start(bf16[16,128,128]{2,1,0:T(8,128)(2,1)} %get-tuple-element.76), channel_id=1, source_target_pairs={{0,12},{4,0},{8,4},{12,8},{1,13},{5,1},{9,5},{13,9},{2,14},{6,2},{... | collective-permute-start | bytes 1572872 | tf_op jit(solution)/shard_map/ppermute | solution.py:20
  168.9 53.6 %all-to-all-start.4 = ((bf16[4,1024,128]{1,2,0:T(8,128)(2,1)}), bf16[4,1024,128]{1,2,0:T(8,128)(2,1)}, u32[]{:S(2)}, u32[]{:S(2)}) async-start(bf16[4,1024,128]{1,2,0:T(8,128)(2,1)} %copy.44), calls=%async_computation.4 | async-start | bytes 2097152 | tf_op jit(solution)/shard_map/all_to_all | solution.py:147
  219.4 0.9 copy-start.9
  220.3 0.8 copy-start.11
  222.4 5.2 %copy-start.12 = (bf16[16,128,128]{2,1,0:T(8,128)(2,1)S(1)}, bf16[16,128,128]{2,1,0:T(8,128)(2,1)}, u32[]{:S(2)}) copy-start(bf16[16,128,128]{2,1,0:T(8,128)(2,1)} %copy-done.11) | copy-start | bytes 1572868
  222.4 5.5 %copy-start.10 = (bf16[16,128,128]{2,1,0:T(8,128)(2,1)S(1)}, bf16[16,128,128]{2,1,0:T(8,128)(2,1)}, u32[]{:S(2)}) copy-start(bf16[16,128,128]{2,1,0:T(8,128)(2,1)} %copy-done.9) | copy-start | bytes 1572868
  222.4 29.9 %all-to-all-start.3 = ((bf16[4,1024,128]{1,2,0:T(8,128)(2,1)}), bf16[4,1024,128]{1,2,0:T(8,128)(2,1)}, u32[]{:S(2)}, u32[]{:S(2)}) async-start(bf16[4,1024,128]{1,2,0:T(8,128)(2,1)} %copy.42), calls=%async_computation.3 | async-start | bytes 2097152 | tf_op jit(solution)/shard_map/all_to_all | solution.py:147
  227.6 12.0 %collective-permute-start.6 = (bf16[16,128,128]{2,1,0:T(8,128)(2,1)S(1)}, bf16[16,128,128]{2,1,0:T(8,128)(2,1)S(1)}, u32[]{:S(2)}, u32[]{:S(2)}) collective-permute-start(bf16[16,128,128]{2,1,0:T(8,128)(2,1)S(1)} %copy-done.12), channel_id=1, source_target_pairs={{0,12},{4,0},{8,4},{12,8},{1,13},{5,1},{9,5},{13,9},{2,14},{6,2},{... | collective-permute-start | bytes 1572872 | tf_op jit(solution)/shard_map/ppermute | solution.py:20
  227.9 13.9 %collective-permute-start.7 = (bf16[16,128,128]{2,1,0:T(8,128)(2,1)S(1)}, bf16[16,128,128]{2,1,0:T(8,128)(2,1)S(1)}, u32[]{:S(2)}, u32[]{:S(2)}) collective-permute-start(bf16[16,128,128]{2,1,0:T(8,128)(2,1)S(1)} %copy-done.10), channel_id=1, source_target_pairs={{0,4},{4,8},{8,12},{12,0},{1,5},{5,9},{9,13},{13,1},{2,6},{6,10},{... | collective-permute-start | bytes 1572872 | tf_op jit(solution)/shard_map/ppermute | solution.py:20
  252.3 28.7 %all-to-all-start.5 = ((bf16[4,1024,128]{1,2,0:T(8,128)(2,1)}), bf16[4,1024,128]{1,2,0:T(8,128)(2,1)S(1)}, u32[]{:S(2)}, u32[]{:S(2)}) async-start(bf16[4,1024,128]{1,2,0:T(8,128)(2,1)} %copy.45), calls=%async_computation.5 | async-start | bytes 2097152 | tf_op jit(solution)/shard_map/all_to_all | solution.py:147
  260.1 1.5 copy-start.1
  260.3 1.0 copy-start.15
  263.1 22.5 %copy-start.14 = (bf16[4,512,2,3,2,32]{1,5,4,3,2,0:T(8,128)(2,1)S(1)}, bf16[4,512,2,3,2,32]{1,5,4,3,2,0:T(8,128)(2,1)}, u32[]{:S(2)}) copy-start(bf16[4,512,2,3,2,32]{1,5,4,3,2,0:T(8,128)(2,1)} %copy.39) | copy-start | bytes 4718596
  281.0 20.3 %all-to-all-start.6 = ((bf16[16,128,128]{2,1,0:T(8,128)(2,1)}), bf16[16,128,128]{2,1,0:T(8,128)(2,1)S(1)}, u32[]{:S(2)}, u32[]{:S(2)}) async-start(bf16[16,128,128]{2,1,0:T(8,128)(2,1)} %bitcast.16), calls=%async_computation.6 | async-start | bytes 1048576 | tf_op jit(solution)/shard_map/all_to_all | solution.py:275
  285.6 2.5 copy-start.4
  285.6 2.5 copy-start.16
  285.6 2.5 copy-start.20
  288.2 1.7 copy-start.17
